TPU v7x, 256 devices: a whole 4x4x8 slice. The times are simulated.
256 devices in a mesh: sec: 4 (over x_hi, core), dev: 64 (over z, y, x_lo).
Axes of the slice: x: 4 (x_hi: 2, x_lo: 2; x = x_hi * 2 + x_lo), y: 4, z: 8, core: 2. Of those that a mesh axis runs over, the one named last changes fastest.
Arguments:
- user_features: bfloat16 [262144, 1024], P(('sec', 'dev')), may hold values from -6 to 6
- w_query_in: bfloat16 [1024, 1024], replicated, may hold values from -0.1875 to 0.1875
- w_query_out: bfloat16 [1024, 256], replicated, may hold values from -0.1875 to 0.1875
- quo_table: bfloat16 [8192, 1024], P('dev'), may hold values from -6 to 6
- rem_table: bfloat16 [8192, 1024], P('dev'), may hold values from -6 to 6
- w_item_in: bfloat16 [1024, 1024], replicated, may hold values from -0.1875 to 0.1875
- w_item_out: bfloat16 [1024, 256], replicated, may hold values from -0.1875 to 0.1875
- quo_bucket: int32 [2048], P('dev'), may hold values from 0 to 8191
- rem_bucket: int32 [2048], P('dev'), may hold values from 0 to 8191
- counts: int32 [2048], replicated, may hold values from 1 to 1000
- positive: int32 [262144], P(('sec', 'dev')), may hold values from 0 to 2047
Outputs:
- losses: float32 [262144], P(('sec', 'dev'))
- grad_query_out: float32 [1024, 256], replicated
- grad_item_out: float32 [1024, 256], replicated
All inputs are finite; a program needn't handle non-finite values.
Results may differ from a plain program's by a relative error of at most 0.004.
The roundings to bfloat16 on the way count: a program that leaves them out, or rounds other values in their place, can miss the bound.
Values may be sent and summed in bfloat16 or wider, within the bound.
A program may use at most 128 MiB of HBM per device.

v0:
```python
import jax
import jax.numpy as jnp
from jax import lax
from jax.sharding import PartitionSpec as P

epsilon = 1e-06
softmax_temper = 0.05


def normalize(vectors):
    width = vectors.shape[-1]
    return (
        vectors
        * lax.rsqrt(jnp.mean(vectors * vectors, axis=-1, keepdims=True) + epsilon)
        * width ** (-0.5)
    )


def local(
    user_features,
    w_query_in,
    w_query_out,
    quo_table,
    rem_table,
    w_item_in,
    w_item_out,
    quo_bucket,
    rem_bucket,
    counts,
    positive,
):
    sections = lax.axis_size("sec")
    members = lax.axis_size("dev")
    section = lax.axis_index("sec")
    member = lax.axis_index("dev")
    item_dev = quo_bucket.shape[0]
    quarter = item_dev // sections
    table_dev = quo_table.shape[0]
    hidden_width = w_query_out.shape[0]
    out_width = w_query_out.shape[1]
    quo_all, rem_all = (
        lax.all_gather(quo_bucket, "dev", axis=0, tiled=True),
        lax.all_gather(rem_bucket, "dev", axis=0, tiled=True),
    )
    row_index = jnp.arange(table_dev, dtype=jnp.int32)

    def requested(bucket_all):
        grouped = bucket_all.reshape(members, sections, quarter)
        return lax.dynamic_index_in_dim(grouped, section, 1, keepdims=False) - member * table_dev

    def serve(local_index, table_shard):
        selector = (local_index[..., None] == row_index).astype(jnp.bfloat16)
        return jnp.einsum(
            "npr,re->npe", selector, table_shard, preferred_element_type=jnp.float32
        ).astype(jnp.bfloat16)

    quo_rows, rem_rows = (
        lax.all_to_all(
            serve(requested(quo_all), quo_table), "dev", split_axis=0, concat_axis=0, tiled=True
        ),
        lax.all_to_all(
            serve(requested(rem_all), rem_table), "dev", split_axis=0, concat_axis=0, tiled=True
        ),
    )
    quo_mine = jnp.sum(quo_rows, axis=0, dtype=jnp.float32)
    rem_mine = jnp.sum(rem_rows, axis=0, dtype=jnp.float32)
    embedded = (quo_mine * rem_mine).astype(jnp.bfloat16)
    hidden_item = jax.nn.relu(
        jnp.dot(embedded, w_item_in, preferred_element_type=jnp.float32)
    ).astype(jnp.bfloat16)
    item_raw = jnp.dot(hidden_item, w_item_out, preferred_element_type=jnp.float32)
    item_embedding_rows = normalize(item_raw).astype(jnp.bfloat16)
    block_vectors = lax.all_gather(item_embedding_rows, "sec", axis=0, tiled=True)
    every_item_row = lax.all_gather(block_vectors, "dev", axis=0, tiled=True)
    item_total_count = every_item_row.shape[0]
    hidden_query = jax.nn.relu(
        jnp.dot(user_features, w_query_in, preferred_element_type=jnp.float32)
    ).astype(jnp.bfloat16)
    query_raw = jnp.dot(hidden_query, w_query_out, preferred_element_type=jnp.float32)
    query_embedding_rows = normalize(query_raw).astype(jnp.bfloat16)
    log_frequency = jnp.log(counts.astype(jnp.float32))
    logit_matrix = (
        jnp.einsum(
            "qd,id->qi", query_embedding_rows, every_item_row, preferred_element_type=jnp.float32
        )
        / softmax_temper
        - log_frequency[None, :]
    )
    log_total = jnp.log(jnp.sum(jnp.exp(logit_matrix), axis=1))
    picked = jnp.take_along_axis(logit_matrix, positive[:, None], axis=1)[:, 0]
    losses = log_total - picked
    item_index = jnp.arange(item_total_count, dtype=jnp.int32)
    onehot = (item_index[None, :] == positive[:, None]).astype(jnp.float32)
    logit_gradient = (jnp.exp(logit_matrix - log_total[:, None]) - onehot).astype(jnp.bfloat16)
    query_gradient = (
        jnp.dot(logit_gradient, every_item_row, preferred_element_type=jnp.float32) / softmax_temper
    )
    _, pullback = jax.vjp(normalize, query_raw)
    raw_grad = pullback(query_gradient)[0].astype(jnp.bfloat16)
    query_term = jnp.einsum("qh,qd->hd", hidden_query, raw_grad, preferred_element_type=jnp.float32)
    block_total = lax.psum_scatter(
        jnp.einsum(
            "qi,qd->id", logit_gradient, query_embedding_rows, preferred_element_type=jnp.float32
        )
        / softmax_temper,
        "dev",
        scatter_dimension=0,
        tiled=True,
    )
    item_grand_count = lax.psum_scatter(block_total, "sec", scatter_dimension=0, tiled=True)
    _, item_pullback = jax.vjp(normalize, item_raw)
    item_raw_grad = item_pullback(item_grand_count)[0].astype(jnp.bfloat16)
    item_term = jnp.einsum(
        "ih,id->hd", hidden_item, item_raw_grad, preferred_element_type=jnp.float32
    )
    limit = (hidden_width * out_width / 2) ** 0.5
    query_sum, item_sum = lax.psum((query_term, item_term), ("sec", "dev"))
    total_norm = jnp.sqrt(jnp.sum(query_sum * query_sum) + jnp.sum(item_sum * item_sum))
    factor = limit / jnp.maximum(total_norm, limit)
    grad_query = query_sum * factor
    grad_item = item_sum * factor
    return (losses, grad_query, grad_item)


def solution(mesh):
    in_specs = (
        P(("sec", "dev"), None),
        P(),
        P(),
        P("dev", None),
        P("dev", None),
        P(),
        P(),
        P("dev"),
        P("dev"),
        P(),
        P(("sec", "dev")),
    )
    out_specs = (P(("sec", "dev")), P(), P())
    return jax.shard_map(local, mesh=mesh, in_specs=in_specs, out_specs=out_specs, check_vma=False)
```

profile of v0, /device:TPU:1, one launch (start us, length us, event | category | flops | bytes accessed | tf_op | source)
XLA Modules:
  0.0 1338.2 jit_solution(10520692428714102527)
XLA Ops:
  7.2 1.4 dynamic-slice
  9.3 0.9 dynamic-update-slice.1
  10.2 0.2 reshape.86
  10.4 0.9 dynamic-update-slice
  11.2 0.2 reshape.85
  11.4 258.0 %all-reduce.4 = (s32[64,4,8]{2,1,0:T(4,128)S(1)}, s32[64,4,8]{2,1,0:T(4,128)S(1)}) all-reduce(s32[64,4,8]{2,1,0:T(4,128)S(1)} %reshape.85, s32[64,4,8]{2,1,0:T(4,128)S(1)} %reshape.86), channel_id=1, replica_groups=mesh['sec'=4,'dev'=64] {'dev'}, use_global_device_ids=true, to_apply=%add | all-reduce | flops 4096 | bytes 32768
  269.5 0.1 dynamic-slice_subtract_fusion
  269.5 2.4 convolution_convert_fusion.1
  271.9 4.7 all-to-all-start
  276.6 1.5 convolution_convert_fusion
  278.1 16.6 %all-to-all-done = bf16[64,8,1024]{2,1,0:T(8,128)(2,1)S(1)} async-done(((bf16[64,8,1024]{2,1,0:T(8,128)(2,1)}), bf16[64,8,1024]{2,1,0:T(8,128)(2,1)S(1)}, u32[]{:S(2)}, u32[]{:S(2)}) %all-to-all-start) | async-done | bytes 1048608 | tf_op jit(solution)/shard_map/all_to_all | solution.py:58
  294.6 5.7 all-to-all-start.1
  300.4 0.0 all-gather.2.cloned.1.call-start
  300.4 0.2 convert_reduce_fusion.1
  300.6 17.7 %all-to-all-done.1 = bf16[64,8,1024]{2,1,0:T(8,128)(2,1)} async-done(((bf16[64,8,1024]{2,1,0:T(8,128)(2,1)}), bf16[64,8,1024]{2,1,0:T(8,128)(2,1)}, u32[]{:S(2)}, u32[]{:S(2)}) %all-to-all-start.1) | async-done | bytes 1048608 | tf_op jit(solution)/shard_map/all_to_all | solution.py:61
  318.3 1.4 convert_reduce_fusion
  319.7 2.0 fusion
  321.7 0.3 multiply_reduce_fusion.5
  322.0 0.1 multiply_convert_fusion.5
  322.0 67.1 %all_gather.14 = bf16[32,256]{1,0:T(8,128)(2,1)} all-gather(bf16[8,256]{1,0:T(8,128)(2,1)S(1)} %multiply_convert_fusion.5), channel_id=1, replica_groups=mesh['sec'=4,'dev'=64] {'sec'}, dimensions={0}, use_global_device_ids=true | all-gather | bytes 20480 | tf_op jit(solution)/shard_map/all_gather | solution.py:73
  389.1 0.0 all-gather.2.cloned.1.call-update
  389.1 0.2 reduce-scatter.3.cloned.1.call-start
  389.4 4.0 maximum_convert_fusion
  393.5 0.8 multiply_reduce_fusion.3
  394.2 0.6 copy-done.1
  394.9 240.3 %all-gather.2.cloned.1.call-done = bf16[2048,256]{1,0:T(8,128)(2,1)} async-done(((bf16[32,256]{1,0:T(8,128)(2,1)}), bf16[2048,256]{1,0:T(8,128)(2,1)}) %all-gather.2.cloned.1.call-update) | async-done | bytes 1048592 | tf_op jit(solution)/shard_map/all_gather | solution.py:74
  635.2 6.3 exponential_reduce_fusion
  641.5 13.4 gather_fusion
  654.8 0.6 fusion.22
  655.4 4.7 subtract_convert_fusion
  660.2 1.9 copy-done.3
  662.1 2.7 convolution_multiply_fusion
  664.8 0.0 reduce-scatter.3.cloned.1.call-update
  664.8 0.0 reduce-scatter.5.cloned.1.call-start
  664.8 4.8 multiply_reduce_fusion.2
  669.6 306.2 %reduce-scatter.3.cloned.1.call-done = f32[32,256]{1,0:T(8,128)} async-done(((f32[2048,256]{1,0:T(8,128)}), f32[32,256]{1,0:T(8,128)}) %reduce-scatter.3.cloned.1.call-update) | async-done | bytes 32784 | tf_op jit(solution)/shard_map/reduce_scatter | solution.py:101
  975.9 0.0 reduce-scatter.5.cloned.1.call-update
  975.9 0.0 all-reduce.8.cloned.1.call-start
  975.9 3.7 fusion.2
  979.6 76.8 %reduce-scatter.5.cloned.1.call-done = f32[8,256]{1,0:T(8,128)} async-done(((f32[32,256]{1,0:T(8,128)}), f32[8,256]{1,0:T(8,128)}) %reduce-scatter.5.cloned.1.call-update) | async-done | bytes 8208 | tf_op jit(solution)/shard_map/reduce_scatter | solution.py:110
  1056.4 0.8 multiply_reduce_fusion.4
  1057.2 2.0 fusion.11
  1059.2 0.0 all-reduce.8.cloned.1.call-update
  1059.2 263.5 %all-reduce.8.cloned.1.call-done = (f32[1024,256]{1,0:T(8,128)}, f32[1024,256]{1,0:T(8,128)}) async-done(((f32[1024,256]{1,0:T(8,128)}, f32[1024,256]{1,0:T(8,128)}), (f32[1024,256]{1,0:T(8,128)}, f32[1024,256]{1,0:T(8,128)})) %all-reduce.8.cloned.1.call-update) | async-done | bytes 2097168 | tf_op jit(solution)/shard_map/psum | solution.py:117
  1322.7 2.2 multiply_reduce_fusion
  1324.9 2.1 multiply_reduce_fusion.1
  1328.4 2.3 broadcast_multiply_fusion
  1330.7 1.0 broadcast_multiply_fusion.1
  (27 shorter events, 0.1 us)
Async XLA Ops:
  7.2 382.3 %copy-start = (bf16[1024,1024]{1,0:T(8,128)(2,1)S(1)}, bf16[1024,1024]{1,0:T(8,128)(2,1)}, u32[]{:S(2)}) copy-start(bf16[1024,1024]{1,0:T(8,128)(2,1)} %param.11) | copy-start | bytes 6291460
  7.2 269.4 %copy-start.6 = (bf16[128,1024]{1,0:T(8,128)(2,1)S(1)}, bf16[128,1024]{1,0:T(8,128)(2,1)}, u32[]{:S(2)}) copy-start(bf16[128,1024]{1,0:T(8,128)(2,1)} %param.15) | copy-start | bytes 786436
  271.9 22.7 %all-to-all-start = ((bf16[64,8,1024]{2,1,0:T(8,128)(2,1)}), bf16[64,8,1024]{2,1,0:T(8,128)(2,1)S(1)}, u32[]{:S(2)}, u32[]{:S(2)}) async-start(bf16[64,8,1024]{2,1,0:T(8,128)(2,1)} %convolution_convert_fusion.1), calls=%async_computation | async-start | bytes 2097152 | tf_op jit(solution)/shard_map/all_to_all | solution.py:58
  294.6 23.6 %all-to-all-start.1 = ((bf16[64,8,1024]{2,1,0:T(8,128)(2,1)}), bf16[64,8,1024]{2,1,0:T(8,128)(2,1)}, u32[]{:S(2)}, u32[]{:S(2)}) async-start(bf16[64,8,1024]{2,1,0:T(8,128)(2,1)} %convolution_convert_fusion), calls=%async_computation.1 | async-start | bytes 2097152 | tf_op jit(solution)/shard_map/all_to_all | solution.py:61
  300.4 334.8 %all-gather.2.cloned.1.call-start = ((), (), s32[]{:S(2)}) async-start(), calls=%async_computation.4 | async-start | bytes 1064960 | tf_op jit(solution)/shard_map/all_gather | solution.py:74
  300.6 21.1 %copy-start.4 = (bf16[1024,256]{1,0:T(8,128)(2,1)S(1)}, bf16[1024,256]{1,0:T(8,128)(2,1)}, u32[]{:S(2)}) copy-start(bf16[1024,256]{1,0:T(8,128)(2,1)} %param.17) | copy-start | bytes 1572868
  300.6 88.8 %copy-start.7 = (s32[1024]{0:T(1024)S(1)}, s32[1024]{0:T(1024)}, u32[]{:S(2)}) copy-start(s32[1024]{0:T(1024)} %param.21) | copy-start | bytes 12292
  389.1 586.7 %reduce-scatter.3.cloned.1.call-start = ((), (), s32[]{:S(2)}) async-start(), calls=%async_computation.5 | async-start | bytes 2129920 | tf_op jit(solution)/shard_map/reduce_scatter | solution.py:101
  389.4 4.0 copy-start.5
  393.4 1.4 copy-start.1
  393.4 1.4 copy-start.8
  660.1 1.9 copy-start.3
  664.8 391.6 %reduce-scatter.5.cloned.1.call-start = ((), (), s32[]{:S(2)}) async-start(), calls=%async_computation.6 | async-start | bytes 40960 | tf_op jit(solution)/shard_map/reduce_scatter | solution.py:110
  975.9 346.9 %all-reduce.8.cloned.1.call-start = ((), (), s32[]{:S(2)}) async-start(), calls=%async_computation.7 | async-start | bytes 4194304 | tf_op jit(solution)/shard_map/psum | solution.py:117
  1322.7 7.9 copy-start.2
Sparse Core Ops, SparseCore 0:
  389.2 245.8 all-gather.1
  664.9 310.8 reduce-scatter.2
  978.7 77.6 reduce-scatter.4
  1062.4 260.3 all-reduce.7
where the time goes:
time: 1340 us
  waiting for transfers between devices  921 us (69%)
  blocking collectives  325 us (24%)
  matrix products  30.3 us (2%)
  local copies, waits for them, and re-layouts  19.5 us (1%)
  between operations  16 us (1%)
  other arithmetic  15.5 us (1%)
    reduce_scatter x1, waiting for transfers between devices, local(): lax.psum_scatter(jnp.einsum('qi,qd->id', logit_gradient, query_embedding_...  306 us
    psum x1, waiting for transfers between devices, local(): query_sum, item_sum = lax.psum((query_term, item_term), ('sec', 'dev'))  264 us
    unnamed x1, blocking collectives  258 us
    all_gather x1, waiting for transfers between devices, local(): every_item_row = lax.all_gather(block_vectors, 'dev', axis=0, tiled=True)  240 us
    reduce_scatter x1, waiting for transfers between devices, local(): lax.psum_scatter(block_total, 'sec', scatter_dimension=0, tiled=True)  76.8 us
    all_gather x1, blocking collectives, local(): lax.all_gather(item_embedding_rows, 'sec', axis=0, tiled=True)  67.1 us
  transfers between devices with their start and end apart: 6, of which 6 were waited for; matrix products, arithmetic and copies ran while one was open for 1% of the time, Pallas kernels for 0%

commit v1 on v0

v1 whole, which is shorter than its diff:
```python
import jax
import jax.numpy as jnp
from jax import lax
from jax.experimental import pallas as pl
from jax.experimental.pallas import tpu as pltpu
from jax.sharding import PartitionSpec as P

EPS = 1e-06
INV_TEMPER = 20.0
MESH = pl.DeviceIdType.MESH
F32 = jnp.float32
BF16 = jnp.bfloat16

NX, NC, NY, NZ = 4, 2, 4, 8
PLANE = NY * NZ
TOK, DIN, HID, DOUT = 1024, 1024, 1024, 256
QUARTER = 8
BLOCK = PLANE * QUARTER
SLOTS = NX * NC
SHARD = 128
TROWS = 8192
CHUNKS = 4
WIDE = DIN // CHUNKS
TILE = 256


def dot(a, b, ca, cb):
    return lax.dot_general(a, b, (((ca,), (cb,)), ((), ())), preferred_element_type=F32)


def norm_parts(raw):
    r = lax.rsqrt(jnp.mean(raw * raw, axis=-1, keepdims=True) + EPS)
    return r


def norm_vjp(raw, grad):
    r = norm_parts(raw)
    dotted = jnp.mean(grad * raw, axis=-1, keepdims=True)
    return (grad * r - raw * (r * r * r * dotted)) * (DOUT**-0.5)


def kernel(
    idx_in, feat_hbm, wqi_hbm, wqo_hbm, quo_hbm, rem_hbm, wii_hbm, wio_hbm, lc_ref, pos_ref,
    loss_ref, gq_ref, gi_ref,
    feat, wqi, wqo, tab, wii, wio,
    idx_recv, idx_sum, srow, rrow, zrow, rzrow,
    hq, qraw, qv, xall, gz, hz, h256,
    est, esum, psum, inv_ref, gall, tsrc, rc, sx, rx, sy, ry, sz, rz,
    rgz, rgy, araw, asrc, arc, asx, arx,
    qsrc, qrc, qsx, qrx, qsy, qry, qz, qy,
    fin, nrm,
    load_sem,
    idx_ss, idx_rs, tab_ss, tab_rs, ry_ss, ry_rs, rz_ss, rz_rs,
    vz_ss, vz_rs, vy_ss, vy_rs, vx_ss, vx_rs, vc_ss, vc_rs,
    hz_ss, hz_rs, hy_ss, hy_rs,
    tc_ss, tc_rs, tx_ss, tx_rs, ty_ss, ty_rs, tz_ss, tz_rs,
    gz_ss, gz_rs, gy_ss, gy_rs,
    ac_ss, ac_rs, ax_ss, ax_rs,
    qc_ss, qc_rs, qx_ss, qx_rs, qyr_ss, qyr_rs, qz_ss, qz_rs, qyg_ss, qyg_rs,
    fx_ss, fx_rs, fc_ss, fc_rs, n_ss, n_rs,
):
    sec = lax.axis_index("sec")
    dev = lax.axis_index("dev")
    xh, c = sec // 2, sec % 2
    z, y, xl = dev // 8, (dev // 2) % 4, dev % 2
    x = xh * 2 + xl
    slot = x * 2 + c
    oc = 1 - c

    def at(ax, ac, ay, az):
        return ((ax // 2) * 2 + ac, (az * NY + ay) * 2 + ax % 2)

    def zp(k):
        return at(x, c, y, (z + k) % NZ)

    def yp(k):
        return at(x, c, (y + k) % NY, z)

    def xp(k):
        return at((x + k) % NX, c, y, z)

    other = at(x, oc, y, z)
    plane = [(ky, kz) for ky in range(NY) for kz in range(NZ) if ky or kz]
    column = [(kx, kc) for kx in range(NX) for kc in range(NC) if kx or kc]
    partner_x = jnp.where(c == 0, x + 1 - 2 * (x % 2), (x + 3 + 2 * (x % 2)) % NX)
    partner = at(partner_x, c, y, z)

    def push(src, dst, ss, rs, target):
        cp = pltpu.make_async_remote_copy(
            src_ref=src, dst_ref=dst, send_sem=ss, recv_sem=rs, device_id=target, device_id_type=MESH
        )
        cp.start()
        return cp

    barrier = pltpu.get_barrier_semaphore()
    for ky, kz in plane:
        pl.semaphore_signal(
            barrier, inc=1, device_id=at(x, c, (y + ky) % NY, (z + kz) % NZ), device_id_type=MESH
        )
    for kx, kc in column:
        pl.semaphore_signal(
            barrier, inc=1, device_id=at((x + kx) % NX, (c + kc) % NC, y, z), device_id_type=MESH
        )

    loads = []
    for i, (src, dst) in enumerate(
        [
            (quo_hbm, tab.at[0]),
            (rem_hbm, tab.at[2]),
            (feat_hbm, feat),
            (wqi_hbm, wqi),
            (wqo_hbm, wqo),
            (wii_hbm, wii),
            (wio_hbm, wio),
        ]
    ):
        cp = pltpu.make_async_copy(src, dst, load_sem.at[i])
        cp.start()
        loads.append(cp)
    pl.semaphore_wait(barrier, len(plane) + len(column))

    idx_cp = []
    for i, (ky, kz) in enumerate(plane):
        idx_cp.append(
            push(
                idx_in,
                idx_recv.at[i],
                idx_ss.at[i],
                idx_rs.at[i],
                at(x, c, (y + ky) % NY, (z + kz) % NZ),
            )
        )
    tab_cp = [
        push(quo_hbm, tab.at[1], tab_ss.at[0], tab_rs.at[0], partner),
        push(rem_hbm, tab.at[3], tab_ss.at[1], tab_rs.at[1], partner),
    ]

    loads[2].wait()
    loads[3].wait()
    for r in range(TOK // TILE):
        rows = pl.ds(r * TILE, TILE)

        @pl.loop(0, HID // TILE)
        def _(j):
            cols = pl.ds(pl.multiple_of(j * TILE, TILE), TILE)
            h = dot(feat[rows, :], wqi[:, cols], 1, 0)
            hq[rows, cols] = jnp.maximum(h, 0.0).astype(BF16)

    for cp in idx_cp:
        cp.wait()
    total = idx_in[...]
    for i in range(len(plane)):
        total = total + idx_recv[i]
    idx_sum[...] = total
    loads[0].wait()
    loads[1].wait()
    for cp in tab_cp:
        cp.wait()
    line = lax.broadcasted_iota(jnp.int32, (4 * SHARD, 128), 0)
    which = line // SHARD
    pair_dev = dev + 1 - 2 * xl
    owner = jnp.where(which % 2 == 0, dev, pair_dev)
    row_id = line % SHARD + owner * SHARD + (which // 2) * TROWS
    tables = tab[...].reshape(4 * SHARD, DIN)

    row_cp = [[None] * NY for _ in range(CHUNKS)]
    for k in (1, 3, 2, 0):
        yy = (y + k) % NY
        wanted = idx_sum[pl.ds(yy, 1), :]
        sel = (row_id == wanted).astype(F32).astype(BF16)
        for ch in range(CHUNKS):
            got = dot(sel, tables[:, ch * WIDE : (ch + 1) * WIDE], 0, 0)
            srow[ch, k] = got.astype(BF16)
    for ch in range(CHUNKS):
        for k in (1, 3, 2):
            row_cp[ch][k] = push(
                srow.at[ch, k], rrow.at[ch, k - 1], ry_ss.at[ch, k - 1], ry_rs.at[ch, k - 1], yp(k)
            )

    loads[4].wait()
    for r in range(TOK // TILE):
        rows = pl.ds(r * TILE, TILE)
        raw = dot(hq[rows, :], wqo[...], 1, 0)
        qraw[rows, :] = raw
        qv[rows, :] = (raw * norm_parts(raw) * (DOUT**-0.5)).astype(BF16)

    zrow_cp = [[None] * NZ for _ in range(CHUNKS)]
    for ch in range(CHUNKS):
        for k in (1, 3, 2):
            row_cp[ch][k].wait()
        s = srow[ch, 0].astype(F32)
        for k in range(NY - 1):
            s = s + rrow[ch, k].astype(F32)
        zrow[ch] = s.astype(BF16).reshape(NZ, 16, WIDE)
        for k in range(1, NZ):
            zrow_cp[ch][k] = push(
                zrow.at[ch, (z + k) % NZ],
                rzrow.at[ch, k - 1],
                rz_ss.at[ch, k - 1],
                rz_rs.at[ch, k - 1],
                zp(k),
            )

    loads[5].wait()
    loads[6].wait()
    pre = jnp.zeros((16, HID), F32)
    for ch in range(CHUNKS):
        for k in range(1, NZ):
            zrow_cp[ch][k].wait()
        s = zrow[ch, z].astype(F32)
        for k in range(NZ - 1):
            s = s + rzrow[ch, k].astype(F32)
        emb = s[:8] * s[8:]
        emb = jnp.concatenate([emb, emb], axis=0).astype(BF16)
        pre = pre + dot(emb, wii[ch * WIDE : (ch + 1) * WIDE, :], 1, 0)
    hid = jnp.maximum(pre, 0.0).astype(BF16)
    iraw = dot(hid, wio[...], 1, 0)[:8]
    ivec = (iraw * norm_parts(iraw) * (DOUT**-0.5)).astype(BF16).astype(F32)
    gz[z] = ivec

    v_cp = []
    for k in range(1, NZ):
        v_cp.append(push(gz.at[z], gz.at[z], vz_ss.at[k - 1], vz_rs.at[k - 1], zp(k)))
    hid8 = hid.astype(F32)[:8]
    hz[z] = jnp.concatenate([hid8[:, :512], hid8[:, 512:]], axis=0).astype(BF16)
    hz_cp = []
    for k in range(1, NZ):
        hz_cp.append(push(hz.at[z], hz.at[z], hz_ss.at[k - 1], hz_rs.at[k - 1], zp(k)))
    for cp in v_cp:
        cp.wait()
    xall[slot, y] = gz[...].reshape(64, DOUT).astype(BF16)
    v_cp = []
    for k in range(1, NY):
        v_cp.append(push(xall.at[slot, y], xall.at[slot, y], vy_ss.at[k - 1], vy_rs.at[k - 1], yp(k)))
    for cp in v_cp:
        cp.wait()
    vx_cp = [None]
    for k in (1, 3, 2):
        vx_cp.append(push(xall.at[slot], xall.at[slot], vx_ss.at[k - 1], vx_rs.at[k - 1], xp(k)))
    vx_cp = [None, vx_cp[1], vx_cp[3], vx_cp[2]]
    vc_cp = [push(xall.at[slot], xall.at[slot], vc_ss.at[0], vc_rs.at[0], other)]

    esum[...] = jnp.zeros_like(esum)
    psum[...] = jnp.zeros_like(psum)

    def first_pass(s):
        vec = xall[s].reshape(BLOCK, DOUT)
        log_count = lc_ref[s]

        @pl.loop(0, TOK // TILE)
        def _(r):
            rows = pl.ds(pl.multiple_of(r * TILE, TILE), TILE)
            logit = dot(qv[rows, :], vec, 1, 1) * INV_TEMPER - log_count
            e = jnp.exp(logit)
            est[s, rows, :] = e
            esum[rows, :] += e[:, :128] + e[:, 128:]
            lane = lax.broadcasted_iota(jnp.int32, (TILE, BLOCK), 1) + s * BLOCK
            hit = jnp.where(lane == pos_ref[rows, :], logit, 0.0)
            psum[rows, :] += hit[:, :128] + hit[:, 128:]

    first_pass(slot)
    vc_cp[0].wait()
    first_pass(x * 2 + oc)
    for i, k in enumerate((1, 3, 2)):
        vx_cp[k].wait()
        s = ((x + NX - k) % NX) * 2 + c
        cp = push(xall.at[s], xall.at[s], vc_ss.at[i + 1], vc_rs.at[i + 1], other)
        vc_cp.append(cp)
        first_pass(s)
        cp.wait()
        first_pass(((x + NX - k) % NX) * 2 + oc)

    for cp in hz_cp:
        cp.wait()
    hv = hz[...].astype(F32)
    h256[y, :, :512] = hv[:, :8, :].reshape(64, 512).astype(BF16)
    h256[y, :, 512:] = hv[:, 8:, :].reshape(64, 512).astype(BF16)
    hy_cp = []

    sums = jnp.sum(esum[...], axis=1, keepdims=True)
    picked = jnp.sum(psum[...], axis=1, keepdims=True)
    loss_ref[...] = jnp.log(sums) - picked
    inv_ref[...] = 1.0 / sums

    def second_pass(s):
        @pl.loop(0, TOK // TILE)
        def _(r):
            rows = pl.ds(pl.multiple_of(r * TILE, TILE), TILE)
            p = est[s, rows, :] * inv_ref[rows, :]
            lane = lax.broadcasted_iota(jnp.int32, (TILE, BLOCK), 1) + s * BLOCK
            g = jnp.where(lane == pos_ref[rows, :], p - 1.0, p)
            gall[s, rows, :] = g.astype(BF16)

        return dot(gall[s], qv[...], 0, 0) * INV_TEMPER

    tc_cp = [None] * NX
    for k in (1, 3, 2, 0):
        s = ((x + k) % NX) * 2 + oc
        tsrc[k] = second_pass(s).astype(BF16)
        tc_cp[k] = push(tsrc.at[k], rc.at[k], tc_ss.at[k], tc_rs.at[k], other)
    tx_cp = []
    own = None
    for k in (1, 3, 2, 0):
        t = second_pass(((x + k) % NX) * 2 + c)
        tc_cp[k].wait()
        t = t + rc[k].astype(F32)
        if k:
            sx[k - 1] = t.astype(BF16)
            tx_cp.append(push(sx.at[k - 1], rx.at[k - 1], tx_ss.at[k - 1], tx_rs.at[k - 1], xp(k)))
        else:
            own = t
    sx[3] = own.astype(BF16)

    for k in range(1, NY):
        hy_cp.append(push(h256.at[y], h256.at[y], hy_ss.at[k - 1], hy_rs.at[k - 1], yp(k)))

    @pl.loop(0, TOK // TILE)
    def _(r):
        rows = pl.ds(pl.multiple_of(r * TILE, TILE), TILE)
        acc = jnp.zeros((TILE, DOUT), F32)
        for s in range(SLOTS):
            acc = acc + dot(gall[s, rows, :], xall[s].reshape(BLOCK, DOUT), 1, 0)
        qv[rows, :] = norm_vjp(qraw[rows, :], acc * INV_TEMPER).astype(BF16)

    def query_part(half):
        return dot(hq[:, pl.ds(pl.multiple_of(half * 512, 512), 512)], qv[...], 0, 0)

    qsrc[...] = query_part(oc).astype(BF16)
    qc_cp = push(qsrc, qrc, qc_ss.at[0], qc_rs.at[0], other)
    qown = query_part(c)

    for cp in tx_cp:
        cp.wait()
    t = sx[3].astype(F32)
    for k in range(NX - 1):
        t = t + rx[k].astype(F32)
    sy[...] = t.astype(BF16).reshape(NY, 64, DOUT)
    ty_cp = []
    for k in range(1, NY):
        ty_cp.append(push(sy.at[(y + k) % NY], ry.at[k - 1], ty_ss.at[k - 1], ty_rs.at[k - 1], yp(k)))

    qc_cp.wait()
    qown = qown + qrc[...].astype(F32)
    qsx[...] = qown.astype(BF16).reshape(NX, 128, DOUT)
    qx_cp = []
    for k in range(1, NX):
        qx_cp.append(push(qsx.at[(x + k) % NX], qrx.at[k - 1], qx_ss.at[k - 1], qx_rs.at[k - 1], xp(k)))

    for cp in ty_cp:
        cp.wait()
    t = sy[y].astype(F32)
    for k in range(NY - 1):
        t = t + ry[k].astype(F32)
    sz[...] = t.reshape(NZ, 8, DOUT)
    tz_cp = []
    for k in range(1, NZ):
        tz_cp.append(push(sz.at[(z + k) % NZ], rz.at[k - 1], tz_ss.at[k - 1], tz_rs.at[k - 1], zp(k)))

    for cp in qx_cp:
        cp.wait()
    q = qsx[x].astype(F32)
    for k in range(NX - 1):
        q = q + qrx[k].astype(F32)
    qsy[...] = q.astype(BF16).reshape(NY, 32, DOUT)
    qy_cp = []
    for k in range(1, NY):
        qy_cp.append(
            push(qsy.at[(y + k) % NY], qry.at[k - 1], qyr_ss.at[k - 1], qyr_rs.at[k - 1], yp(k))
        )

    for cp in tz_cp:
        cp.wait()
    t = sz[z]
    for k in range(NZ - 1):
        t = t + rz[k]
    rgz[z] = norm_vjp(iraw, t).astype(BF16).astype(F32)
    g_cp = []
    for k in range(1, NZ):
        g_cp.append(push(rgz.at[z], rgz.at[z], gz_ss.at[k - 1], gz_rs.at[k - 1], zp(k)))

    for cp in qy_cp:
        cp.wait()
    q = qsy[y].astype(F32)
    for k in range(NY - 1):
        q = q + qry[k].astype(F32)
    qz[z] = q.astype(BF16)
    qz_cp = []
    for k in range(1, NZ):
        qz_cp.append(push(qz.at[z], qz.at[z], qz_ss.at[k - 1], qz_rs.at[k - 1], zp(k)))

    for cp in g_cp:
        cp.wait()
    rgy[y] = rgz[...].reshape(64, DOUT).astype(BF16)
    g_cp = []
    for k in range(1, NY):
        g_cp.append(push(rgy.at[y], rgy.at[y], gy_ss.at[k - 1], gy_rs.at[k - 1], yp(k)))

    for cp in qz_cp:
        cp.wait()
    q = qz[0].astype(F32)
    for k in range(1, NZ):
        q = q + qz[k].astype(F32)
    qy[y] = q.astype(BF16)
    qy_cp = []
    for k in range(1, NY):
        qy_cp.append(push(qy.at[y], qy.at[y], qyg_ss.at[k - 1], qyg_rs.at[k - 1], yp(k)))

    for cp in hy_cp:
        cp.wait()
    for cp in g_cp:
        cp.wait()
    rg = rgy[...].reshape(BLOCK, DOUT)

    def item_part(half):
        cols = pl.ds(pl.multiple_of(half * 512, 512), 512)
        return dot(h256[:, :, cols].reshape(BLOCK, 512), rg, 0, 0)

    asrc[...] = item_part(oc).astype(BF16)
    ac_cp = push(asrc, arc, ac_ss.at[0], ac_rs.at[0], other)
    araw[...] = item_part(c)
    ac_cp.wait()
    asx[...] = (araw[...] + arc[...].astype(F32)).astype(BF16).reshape(NX, 128, DOUT)
    ax_cp = []
    for k in range(1, NX):
        ax_cp.append(push(asx.at[(x + k) % NX], arx.at[k - 1], ax_ss.at[k - 1], ax_rs.at[k - 1], xp(k)))
    for cp in qy_cp:
        cp.wait()
    fin[slot, 0] = qy[...].reshape(128, DOUT)
    for cp in ax_cp:
        cp.wait()
    a = asx[x].astype(F32)
    for k in range(NX - 1):
        a = a + arx[k].astype(F32)
    fin[slot, 1] = a.astype(BF16)
    mine = fin[slot].astype(F32)
    square = mine * mine
    square = jnp.sum(square.reshape(2 * 128 // 8, 8, DOUT), axis=0)
    nrm[slot] = square[:, :128] + square[:, 128:]

    fx_cp = [None] * NX
    for k in (1, 3, 2):
        fx_cp[k] = push(fin.at[slot], fin.at[slot], fx_ss.at[k - 1], fx_rs.at[k - 1], xp(k))
    n_cp = []
    for i, (kx, kc) in enumerate(column):
        n_cp.append(
            push(
                nrm.at[slot], nrm.at[slot], n_ss.at[i], n_rs.at[i],
                at((x + kx) % NX, (c + kc) % NC, y, z),
            )
        )
    fc_cp = [push(fin.at[slot], fin.at[slot], fc_ss.at[0], fc_rs.at[0], other)]
    for cp in n_cp:
        cp.wait()
    square = nrm[0]
    for s in range(1, SLOTS):
        square = square + nrm[s]
    norm = jnp.sqrt(jnp.sum(jnp.sum(square, axis=1, keepdims=True), axis=0, keepdims=True))
    limit = (HID * DOUT / 2) ** 0.5
    factor = limit / jnp.maximum(norm, limit)

    def put(s):
        at_row = pl.ds(pl.multiple_of((s % 2) * 512 + (s // 2) * 128, 128), 128)
        gq_ref[at_row, :] = fin[s, 0].astype(F32) * factor
        gi_ref[at_row, :] = fin[s, 1].astype(F32) * factor

    put(slot)
    for i, k in enumerate((1, 3, 2)):
        fx_cp[k].wait()
        s = ((x + NX - k) % NX) * 2 + c
        fc_cp.append(push(fin.at[s], fin.at[s], fc_ss.at[i + 1], fc_rs.at[i + 1], other))
        put(s)
    fc_cp[0].wait()
    put(x * 2 + oc)
    for i, k in enumerate((1, 3, 2)):
        fc_cp[i + 1].wait()
        put(((x + NX - k) % NX) * 2 + oc)


def local(
    user_features, w_query_in, w_query_out, quo_table, rem_table, w_item_in, w_item_out,
    quo_bucket, rem_bucket, counts, positive,
):
    sec = lax.axis_index("sec")
    dev = lax.axis_index("dev")
    z, y = dev // 8, (dev // 2) % 4
    mine = jnp.concatenate(
        [
            lax.dynamic_slice(quo_bucket, (sec * QUARTER,), (QUARTER,)),
            lax.dynamic_slice(rem_bucket, (sec * QUARTER,), (QUARTER,)) + TROWS,
        ]
    )
    requests = lax.dynamic_update_slice(
        jnp.zeros((NY, 128), jnp.int32), mine[None, :], (y, z * 2 * QUARTER)
    )
    log_count = jnp.log(counts.astype(F32)).reshape(NZ, NY, 2, 2, 2, QUARTER)
    log_count = log_count.transpose(3, 2, 4, 1, 0, 5).reshape(SLOTS, 1, BLOCK)
    j = positive % 8
    core, x_hi, x_lo = (positive // 8) % 2, (positive // 16) % 2, (positive // 32) % 2
    py, pz = (positive // 64) % 4, positive // 256
    place = ((((x_hi * 2 + x_lo) * 2 + core) * NY + py) * NZ + pz) * QUARTER + j

    def vm(*shape, dtype=BF16):
        return pltpu.VMEM(shape, dtype)

    def dma(*shape):
        return pltpu.SemaphoreType.DMA(shape)

    anyspace = pl.BlockSpec(memory_space=pl.ANY)
    vmem = pl.BlockSpec(memory_space=pltpu.VMEM)
    scratch = [
        vm(TOK, DIN), vm(DIN, HID), vm(HID, DOUT), vm(4, SHARD, DIN), vm(DIN, HID), vm(HID, DOUT),
        vm(PLANE - 1, NY, 128, dtype=jnp.int32), vm(NY, 128, dtype=jnp.int32),
        vm(CHUNKS, NY, 128, WIDE), vm(CHUNKS, NY - 1, 128, WIDE),
        vm(CHUNKS, NZ, 16, WIDE), vm(CHUNKS, NZ - 1, 16, WIDE),
        vm(TOK, HID), vm(TOK, DOUT, dtype=F32), vm(TOK, DOUT),
        vm(SLOTS, NY, 64, DOUT), vm(NZ, 8, DOUT, dtype=F32), vm(NZ, 16, 512), vm(NY, 64, HID),
        vm(SLOTS, TOK, BLOCK, dtype=F32), vm(TOK, 128, dtype=F32), vm(TOK, 128, dtype=F32),
        vm(TOK, 1, dtype=F32), vm(SLOTS, TOK, BLOCK),
        vm(NX, BLOCK, DOUT), vm(NX, BLOCK, DOUT), vm(NX, BLOCK, DOUT), vm(NX - 1, BLOCK, DOUT),
        vm(NY, 64, DOUT), vm(NY - 1, 64, DOUT), vm(NZ, 8, DOUT, dtype=F32), vm(NZ - 1, 8, DOUT, dtype=F32),
        vm(NZ, 8, DOUT, dtype=F32), vm(NY, 64, DOUT),
        vm(512, DOUT, dtype=F32), vm(512, DOUT), vm(512, DOUT), vm(NX, 128, DOUT), vm(NX - 1, 128, DOUT),
        vm(512, DOUT), vm(512, DOUT), vm(NX, 128, DOUT), vm(NX - 1, 128, DOUT),
        vm(NY, 32, DOUT), vm(NY - 1, 32, DOUT), vm(NZ, 32, DOUT), vm(NY, 32, DOUT),
        vm(SLOTS, 2, 128, DOUT), vm(SLOTS, 8, 128, dtype=F32),
        dma(7),
        dma(31), dma(31), dma(2), dma(2), dma(CHUNKS, 3), dma(CHUNKS, 3), dma(CHUNKS, 7), dma(CHUNKS, 7),
        dma(7), dma(7), dma(3), dma(3), dma(3), dma(3), dma(4), dma(4),
        dma(7), dma(7), dma(3), dma(3),
        dma(4), dma(4), dma(3), dma(3), dma(3), dma(3), dma(7), dma(7),
        dma(7), dma(7), dma(3), dma(3),
        dma(1), dma(1), dma(3), dma(3),
        dma(1), dma(1), dma(3), dma(3), dma(3), dma(3), dma(7), dma(7), dma(3), dma(3),
        dma(3), dma(3), dma(4), dma(4), dma(7), dma(7),
    ]
    losses, grad_query, grad_item = pl.pallas_call(
        kernel,
        out_shape=(
            jax.ShapeDtypeStruct((TOK, 1), F32),
            jax.ShapeDtypeStruct((HID, DOUT), F32),
            jax.ShapeDtypeStruct((HID, DOUT), F32),
        ),
        in_specs=[vmem] + [anyspace] * 7 + [vmem] * 2,
        out_specs=(vmem, vmem, vmem),
        scratch_shapes=scratch,
        compiler_params=pltpu.CompilerParams(
            collective_id=0, has_side_effects=True, vmem_limit_bytes=56 * 2**20
        ),
        cost_estimate=pl.CostEstimate(flops=6_500_000_000, bytes_accessed=12_000_000, transcendentals=2_100_000),
        name="step",
    )(
        requests, user_features, w_query_in, w_query_out, quo_table, rem_table, w_item_in, w_item_out,
        log_count, place[:, None],
    )
    return (losses.reshape(TOK), grad_query, grad_item)


def solution(mesh):
    in_specs = (
        P(("sec", "dev"), None), P(), P(), P("dev", None), P("dev", None), P(), P(),
        P("dev"), P("dev"), P(), P(("sec", "dev")),
    )
    out_specs = (P(("sec", "dev")), P(), P())
    return jax.shard_map(local, mesh=mesh, in_specs=in_specs, out_specs=out_specs, check_vma=False)
```

time: 1340 us -> 128 us (0.10)
  waiting for transfers between devices: 921 us -> 0 us
  blocking collectives: 325 us -> 0 us
  Pallas kernels: 0 us -> 117 us
  matrix products: 30.3 us -> 0 us
  between operations: 16 us -> 0.73 us
    reduce_scatter x2 -> x0, waiting for transfers between devices: 383 us -> none  [the longest x1 306 us: local(): lax.psum_scatter(jnp.einsum('qi,qd->id', logit_gradient, query_embedding_...]
    psum x1 -> x0, waiting for transfers between devices: 264 us -> none  [local(): query_sum, item_sum = lax.psum((query_term, item_term), ('sec', 'dev'))]
    unnamed x1 -> x0, blocking collectives: 258 us -> none
    all_gather x1 -> x0, waiting for transfers between devices: 240 us -> none  [local(): every_item_row = lax.all_gather(block_vectors, 'dev', axis=0, tiled=True)]
    pallas_call x0 -> x1, Pallas kernels: none -> 117 us  [local(): pl.pallas_call(kernel, out_shape=(jax.ShapeDtypeStruct((TOK, 1), F32), ja...]
    all_gather x1 -> x0, blocking collectives: 67.1 us -> none  [local(): lax.all_gather(item_embedding_rows, 'sec', axis=0, tiled=True)]
    all_to_all x2 -> x0, waiting for transfers between devices: 34.2 us -> none  [the longest x1 17.7 us: local(): lax.all_to_all(serve(requested(rem_all), rem_table), 'dev', split_axis=0,...]
    dot_general x11 -> x0, matrix products: 30.3 us -> none  [the longest x1 6.26 us: local(): jnp.einsum('qd,id->qi', query_embedding_rows, every_item_row, preferred_e...]
  transfers between devices with their start and end apart: 6 -> 0, of which waited for: 6 -> 0; matrix products, arithmetic and copies ran while one was open for 1% -> 0% of each run, Pallas kernels for 0% -> 0%
where the time goes in v1:
time: 128 us
  Pallas kernels  117 us (91%)
  local copies, waits for them, and re-layouts  6.13 us (5%)
  other arithmetic  4.16 us (3%)
    pallas_call x1, Pallas kernels, local(): pl.pallas_call(kernel, out_shape=(jax.ShapeDtypeStruct((TOK, 1), F32), ja...  117 us
    unnamed x6, local copies, waits for them, and re-layouts  3.24 us

profile of v1, /device:TPU:1, one launch (start us, length us, event | category | flops | bytes accessed | tf_op | source)
XLA Modules:
  0.0 127.5 jit_solution(3903004615817040144)
XLA Ops:
  0.7 0.7 dynamic_slice.6
  1.4 0.7 dynamic-slice_add_fusion
  2.1 0.1 add_bitcast_fusion
  2.2 0.1 dynamic_update_slice.3.idx_in
  2.3 0.0 copy-start.1
  2.3 0.7 fusion.11
  3.1 0.7 convert_log_fusion
  3.8 0.2 reshape.15
  4.0 0.1 copy.14
  4.1 0.7 reshape.16.lc_ref
  4.8 1.0 copy.15.pos_ref
  5.8 0.0 copy-done.1
  5.8 116.5 %step.1 = (f32[1024,1]{1,0:T(8,128)}, f32[1024,256]{1,0:T(8,128)}, f32[1024,256]{1,0:T(8,128)}) custom-call(s32[4,128]{1,0:T(4,128)} %copy-done.1, bf16[1024,1024]{1,0:T(8,128)(2,1)} %feat_hbm.1, bf16[1024,1024]{1,0:T(8,128)(2,1)} %wqi_hbm.1, bf16[1024,256]{1,0:T(8,128)(2,1)} %wqo_hbm.1, bf16[128,1024]{1,0:T(8,128)(2,1)} %quo_hbm.1, ...), custom_call_target="tpu_custom_call" | custom-call | flops 6499999744 | bytes 12000000 | tf_op jit(solution)/shard_map/step/pallas_call | solution.py:536
  122.4 0.0 copy-start
  122.4 1.9 %reduce = f32[1024]{0:T(1024)} reduce(f32[1024,1]{1,0:T(8,128)} %get-tuple-element.6, f32[]{:T(128)} %constant.146), dimensions={1}, to_apply=%get-tuple-element.6.reduce_sub_computation | reduce | bytes 8196 | tf_op jit(solution)/shard_map/step/pallas_call | solution.py:536
  124.3 2.3 %copy.19 = f32[1024,256]{1,0:T(8,128)} copy(f32[1024,256]{1,0:T(8,128)} %get-tuple-element.13) | data formatting | bytes 2097152
  126.6 0.0 copy-done
  126.6 1.0 copy.20
  (1 shorter events, 0.0 us)
Async XLA Ops:
  2.3 3.5 %copy-start.1 = (s32[4,128]{1,0:T(4,128)}, s32[4,128]{1,0:T(4,128)S(1)}, u32[]{:S(2)}) copy-start(s32[4,128]{1,0:T(4,128)S(1)} %dynamic_update_slice.3.idx_in) | copy-start | bytes 6148
  122.4 4.2 %copy-start = (f32[1024,256]{1,0:T(8,128)S(1)}, f32[1024,256]{1,0:T(8,128)}, u32[]{:S(2)}) copy-start(f32[1024,256]{1,0:T(8,128)} %get-tuple-element.14) | copy-start | bytes 3145732

commit v2 on v0

v2 whole, which is shorter than its diff:
```python
import jax
import jax.numpy as jnp
from jax import lax
from jax.experimental import pallas as pl
from jax.experimental.pallas import tpu as pltpu
from jax.sharding import PartitionSpec as P

EPS = 1e-06
INV_TEMPER = 20.0
LOG2E = 1.4426950408889634
MESH = pl.DeviceIdType.MESH
F32 = jnp.float32
BF16 = jnp.bfloat16

NX, NC, NY, NZ = 4, 2, 4, 8
PLANE = NY * NZ
TOK, DIN, HID, DOUT = 1024, 1024, 1024, 256
QUARTER = 8
BLOCK = PLANE * QUARTER
SLOTS = NX * NC
SHARD = 128
TROWS = 8192
CHUNKS = 4
WIDE = DIN // CHUNKS
TILE = 256
HALF = 128
LINE = 32
ROWS = NC * NX * LINE


def dot(a, b, ca, cb):
    return lax.dot_general(a, b, (((ca,), (cb,)), ((), ())), preferred_element_type=F32)


def norm_scale(raw):
    return lax.rsqrt(jnp.mean(raw * raw, axis=-1, keepdims=True) + EPS)


def norm_vjp(raw, grad):
    r = norm_scale(raw)
    dotted = jnp.mean(grad * raw, axis=-1, keepdims=True)
    return (grad * r - raw * (r * r * r * dotted)) * (DOUT**-0.5)


def stack(rows):
    n = rows.shape[0] // 8
    left = rows[:, :HALF].reshape(n, 8, HALF)
    right = rows[:, HALF:].reshape(n, 8, HALF)
    return jnp.concatenate([left, right], axis=1)


def unstack(tiles):
    n = tiles.shape[0]
    left = tiles[:, :8, :].reshape(n * 8, HALF)
    right = tiles[:, 8:, :].reshape(n * 8, HALF)
    return left, right


def gray(p):
    return p + jnp.where(p == 2, 1, 0) - jnp.where(p == 3, 1, 0)


def kernel(
    quo_idx, rem_idx, feat_hbm, wqi_hbm, wqo_hbm, quo_hbm, rem_hbm, wii_hbm, wio_hbm, counts_in, pos_in,
    loss_ref, fin_query, fin_item, factor_ref,
    feat, wqi, wqo, tab, wii, wio,
    idx_out, idx_recv, sel, srow, rrow, zrow, rzrow, pre,
    hq, qraw, qv, xall, gv, hz, hsrc, hcol,
    est, esum, psum, posb, invb, gall, tsrc, rc, sx, rx, town, sg, rg,
    rgv, arc, aown, asx, arx,
    qfull, qsrc, qrc, qsx, qrx, qsy, qry, qz,
    nrm, nsum, lc_ref,
    load_sem,
    idx_ss, idx_rs, tab_ss, tab_rs, ry_ss, ry_rs, rz_ss, rz_rs,
    vp_ss, vp_rs, vx_ss, vx_rs, vc_ss, vc_rs,
    hz_ss, hz_rs, hy_ss, hy_rs,
    tc_ss, tc_rs, tx_ss, tx_rs, tp_ss, tp_rs,
    gp_ss, gp_rs,
    ac_ss, ac_rs, ax_ss, ax_rs,
    qc_ss, qc_rs, qx_ss, qx_rs, qyr_ss, qyr_rs, qz_ss, qz_rs,
    f_ss, f_rs, fc_ss, fc_rs, n_ss, n_rs, ns_ss, ns_rs,
):
    sec = lax.axis_index("sec")
    dev = lax.axis_index("dev")
    xh, c = sec // 2, sec % 2
    z, y, xl = dev // 8, (dev // 2) % 4, dev % 2
    x = xh * 2 + xl
    slot = x * 2 + c
    mine = y * NZ + z
    oc = 1 - c

    def at(ax, ac, ay, az):
        return ((ax // 2) * 2 + ac, (az * NY + ay) * 2 + ax % 2)

    def zp(k):
        return at(x, c, y, (z + k) % NZ)

    def yp(k):
        return at(x, c, (y + k) % NY, z)

    def xp(k):
        return at((x + k) % NX, c, y, z)

    other = at(x, oc, y, z)
    plane = [(ky, kz) for ky in range(NY) for kz in range(NZ) if ky or kz]
    sheet = [(kx, ky) for ky in range(NY) for kx in range(NX) if kx or ky]

    def sp(kx, ky):
        return at((x + kx) % NX, c, (y + ky) % NY, z)

    def pp(i):
        ky, kz = plane[i]
        return at(x, c, (y + ky) % NY, (z + kz) % NZ)

    def pg(i):
        ky, kz = plane[i]
        return ((y + ky) % NY) * NZ + (z + kz) % NZ

    partner_x = jnp.where(c == 0, x + 1 - 2 * (x % 2), (x + 3 + 2 * (x % 2)) % NX)
    partner = at(partner_x, c, y, z)
    fin = (fin_query, fin_item)
    sent = []

    def copy(src, dst, ss, rs, target):
        return pltpu.make_async_remote_copy(
            src_ref=src, dst_ref=dst, send_sem=ss, recv_sem=rs, device_id=target, device_id_type=MESH
        )

    def push(src, dst, ss, rs, target):
        cp = copy(src, dst, ss, rs, target)
        cp.start()
        sent.append(cp)
        return cp

    barrier = pltpu.get_barrier_semaphore()
    for i in range(len(plane)):
        pl.semaphore_signal(barrier, inc=1, device_id=pp(i), device_id_type=MESH)
    greeted = len(plane) + 1
    pl.semaphore_signal(barrier, inc=1, device_id=other, device_id_type=MESH)
    for kx, ky in sheet:
        if kx:
            greeted += 1
            pl.semaphore_signal(barrier, inc=1, device_id=sp(kx, ky), device_id_type=MESH)

    loads = []
    for i, (src, dst) in enumerate(
        [
            (quo_hbm, tab.at[pl.ds(0, SHARD)]),
            (rem_hbm, tab.at[pl.ds(2 * SHARD, SHARD)]),
            (feat_hbm, feat),
            (wqi_hbm, wqi),
            (wqo_hbm, wqo),
            (wii_hbm, wii),
            (wio_hbm, wio),
        ]
    ):
        cp = pltpu.make_async_copy(src, dst, load_sem.at[i])
        cp.start()
        loads.append(cp)

    lane = lax.broadcasted_iota(jnp.int32, (NY, HALF), 1) - z * 2 * QUARTER
    lane = jnp.where(lax.broadcasted_iota(jnp.int32, (NY, HALF), 0) == y, lane, -1)
    asked = jnp.zeros((NY, HALF), jnp.int32)
    for j in range(QUARTER):
        asked = jnp.where(lane == j, quo_idx[sec * QUARTER + j], asked)
        asked = jnp.where(lane == QUARTER + j, rem_idx[sec * QUARTER + j] + TROWS, asked)
    idx_out[...] = asked
    loads[0].wait()
    loads[1].wait()
    pl.semaphore_wait(barrier, greeted)

    idx_cp = [
        push(idx_out, idx_recv.at[i], idx_ss.at[i], idx_rs.at[i], pp(i)) for i in range(len(plane))
    ]
    own_rows = pl.ds(pl.multiple_of(c * 2 * SHARD, SHARD), SHARD)
    their_rows = pl.ds(pl.multiple_of(c * 2 * SHARD + SHARD, SHARD), SHARD)
    tab_cp = push(tab.at[own_rows], tab.at[their_rows], tab_ss.at[0], tab_rs.at[0], partner)

    pos = pos_in[...]
    place = ((pos // 16) % 2) * 1024 + ((pos // 32) % 2) * 512 + ((pos // 8) % 2) * 256
    place = place + ((pos // 64) % 4) * 64 + (pos // 256) * 8 + pos % 8
    place = place.T
    for i in range(TOK // HALF):
        posb[pl.ds(i * HALF, HALF), :] = jnp.broadcast_to(place[:, i : i + 1], (HALF, HALF))

    counts = counts_in[...]
    high = (counts // 8).astype(F32).astype(BF16)
    low = (counts % 8).astype(F32).astype(BF16)
    src = lax.broadcasted_iota(jnp.int32, (HALF, BLOCK), 0)
    dst = lax.broadcasted_iota(jnp.int32, (HALF, BLOCK), 1)
    src = jnp.where((src // 64 == (dst // 64) % 2) & (src % 8 == dst % 8), (src // 8) % 8, -1)
    down = lax.broadcasted_iota(jnp.int32, (16, BLOCK), 0)
    dst = lax.broadcasted_iota(jnp.int32, (16, BLOCK), 1)
    keep = down == ((dst // 8) % 8) * 2 + dst // HALF
    for s in range(SLOTS):
        pick = (src == (s // 2 % 2) * 4 + (s // 4) * 2 + s % 2).astype(F32).astype(BF16)
        wide = dot(high, pick, 1, 0) * 8.0 + dot(low, pick, 1, 0)
        lc_ref[s] = jnp.log(jnp.sum(jnp.where(keep, wide, 0.0), axis=0, keepdims=True)) * LOG2E

    loads[2].wait()
    loads[3].wait()

    hq[...] = jnp.maximum(dot(feat[...], wqi[...], 1, 0), 0.0).astype(BF16)

    tab_cp.wait_recv()
    tabc_cp = push(tab.at[their_rows], tab.at[their_rows], tab_ss.at[1], tab_rs.at[1], other)
    for cp in idx_cp:
        cp.wait_recv()
    total = idx_out[...]
    for i in range(len(plane)):
        total = total + idx_recv[i]
    total = jnp.concatenate([total, jnp.zeros((8 - NY, HALF), jnp.int32)], axis=0).T
    line = lax.broadcasted_iota(jnp.int32, (HALF, 4 * SHARD), 1)
    which = line // SHARD
    owner = jnp.where(which % 2 == 0, dev, dev + 1 - 2 * xl)
    row_id = line % SHARD + owner * SHARD + (which // 2) * TROWS
    for i in range(NY):
        sel[i] = (row_id == total[:, i : i + 1]).astype(F32).astype(BF16)
    tabc_cp.wait_recv()

    def row_copy(ch, k):
        return copy(srow.at[ch, k], rrow.at[ch, k - 1], ry_ss.at[ch, k - 1], ry_rs.at[ch, k - 1], yp(k))

    @pl.loop(0, CHUNKS)
    def _(ch):
        cols = pl.ds(pl.multiple_of(ch * WIDE, WIDE), WIDE)
        for k in (1, 3, 2, 0):
            srow[ch, k] = dot(sel[(y + k) % NY], tab[:, cols], 1, 0).astype(BF16)
            if k:
                row_copy(ch, k).start()

    loads[4].wait()

    raw = dot(hq[...], wqo[...], 1, 0)
    qraw[...] = raw
    qv[...] = (raw * norm_scale(raw) * (DOUT**-0.5)).astype(BF16)

    def zrow_copy(ch, k):
        return copy(
            zrow.at[ch, (z + k) % NZ], rzrow.at[ch, k - 1], rz_ss.at[ch, k - 1], rz_rs.at[ch, k - 1], zp(k)
        )

    @pl.loop(0, CHUNKS)
    def _(ch):
        for k in (1, 3, 2):
            row_copy(ch, k).wait_recv()
        s = srow[ch, 0].astype(F32)
        for k in range(NY - 1):
            s = s + rrow[ch, k].astype(F32)
        zrow[ch] = s.astype(BF16).reshape(NZ, 16, WIDE)
        for k in range(1, NZ):
            zrow_copy(ch, k).start()

    loads[5].wait()
    loads[6].wait()
    pre[...] = jnp.zeros_like(pre)

    @pl.loop(0, CHUNKS)
    def _(ch):
        for k in range(1, NZ):
            zrow_copy(ch, k).wait_recv()
        s = zrow[ch, z].astype(F32)
        for k in range(NZ - 1):
            s = s + rzrow[ch, k].astype(F32)
        emb = s[:8] * s[8:]
        emb = jnp.concatenate([emb, emb], axis=0).astype(BF16)
        rows = pl.ds(pl.multiple_of(ch * WIDE, WIDE), WIDE)
        pre[...] += dot(emb, wii[rows, :], 1, 0)

    hid = jnp.maximum(pre[...], 0.0).astype(BF16)
    iraw = dot(hid, wio[...], 1, 0)[:8]
    ivec = iraw * norm_scale(iraw) * (DOUT**-0.5)
    gv[mine] = stack(ivec)[0].astype(BF16)

    v_cp = [
        push(gv.at[mine], gv.at[mine], vp_ss.at[i], vp_rs.at[i], pp(i)) for i in range(len(plane))
    ]
    hid8 = hid.astype(F32)[:8]
    hz[z] = jnp.concatenate([hid8[:, :512], hid8[:, 512:]], axis=0).astype(BF16)
    esum[...] = jnp.zeros_like(esum)
    psum[...] = jnp.zeros_like(psum)
    for cp in v_cp:
        cp.wait_recv()
    left, right = unstack(gv[...].astype(F32))
    xall[slot, :, :HALF] = left.astype(BF16)
    xall[slot, :, HALF:] = right.astype(BF16)

    def vx_copy(k):
        return copy(xall.at[slot], xall.at[slot], vx_ss.at[k - 1], vx_rs.at[k - 1], xp(k))

    for k in (1, 3, 2):
        vx_copy(k).start()
    hz_cp = [
        push(hz.at[z], hz.at[z], hz_ss.at[k - 1], hz_rs.at[k - 1], zp(k)) for k in range(1, NZ)
    ]

    def first_pass(s):
        logit = dot(qv[...], xall[s], 1, 1) * (INV_TEMPER * LOG2E) - lc_ref[s]
        e = jnp.exp2(logit)
        est[s] = e
        esum[...] += e[:, :HALF] + e[:, HALF:]
        lanes = lax.broadcasted_iota(jnp.int32, (TOK, HALF), 1)
        target = posb[...] - s * BLOCK
        hit = jnp.where(target == lanes, logit[:, :HALF], 0.0)
        hit = jnp.where(target == lanes + HALF, logit[:, HALF:], hit)
        psum[...] += hit

    def vc_copy(p):
        s = ((x + NX - gray(p)) % NX) * 2 + c
        return copy(xall.at[s], xall.at[s], vc_ss.at[p], vc_rs.at[p], other)

    @pl.loop(0, NX)
    def _(p):
        @pl.when(p > 0)
        def _():
            vx_copy(gray(p)).wait_recv()

        s = ((x + NX - gray(p)) % NX) * 2
        vc_copy(p).start()
        first_pass(s + c)
        vc_copy(p).wait_recv()
        first_pass(s + oc)

    for cp in hz_cp:
        cp.wait_recv()
    hv = hz[...].astype(F32)
    hv = jnp.concatenate([hv[:, :8, :].reshape(64, 512), hv[:, 8:, :].reshape(64, 512)], axis=1)
    hv = hv.astype(BF16)
    for i in range(NY):
        hsrc[i] = hv[:, i * ROWS : (i + 1) * ROWS]
    hcol[y] = hsrc[y]
    hy_cp = [
        push(hsrc.at[(y + k) % NY], hcol.at[y], hy_ss.at[k - 1], hy_rs.at[k - 1], yp(k))
        for k in range(1, NY)
    ]
    sums = jnp.sum(esum[...], axis=1, keepdims=True)
    picked = jnp.sum(psum[...], axis=1, keepdims=True)
    invb[...] = jnp.broadcast_to(1.0 / sums, (TOK, HALF))
    loss = (jnp.log2(sums) - picked) * (1.0 / LOG2E)
    loss = jnp.broadcast_to(loss, (TOK, HALF)).reshape(TOK // HALF, HALF, HALF)
    down = lax.broadcasted_iota(jnp.int32, (TOK // HALF, HALF, HALF), 1)
    across = lax.broadcasted_iota(jnp.int32, (TOK // HALF, HALF, HALF), 2)
    loss_ref[...] = jnp.sum(jnp.where(down == across, loss, 0.0), axis=1)

    def weigh(s):
        lanes = lax.broadcasted_iota(jnp.int32, (TOK, HALF), 1)
        target = posb[...] - s * BLOCK
        scale = invb[...]
        pa = est[s, :, :HALF] * scale
        pb = est[s, :, HALF:] * scale
        gall[s, :, :HALF] = jnp.where(target == lanes, pa - 1.0, pa).astype(BF16)
        gall[s, :, HALF:] = jnp.where(target == lanes + HALF, pb - 1.0, pb).astype(BF16)

    def spread(s):
        return dot(gall[s], qv[...], 0, 0) * INV_TEMPER

    def tc_copy(k):
        return copy(tsrc.at[k], rc.at[k], tc_ss.at[k], tc_rs.at[k], other)

    def tx_copy(k):
        return copy(sx.at[k], rx.at[k - 1], tx_ss.at[k - 1], tx_rs.at[k - 1], xp(k))

    @pl.loop(0, NX)
    def _(p):
        k = gray((p + 1) % NX)
        s = ((x + k) % NX) * 2
        weigh(s + oc)
        weigh(s + c)
        tsrc[k] = spread(s + oc).astype(BF16)
        tc_copy(k).start()
        t = spread(s + c)
        tc_copy(k).wait_recv()
        t = t + rc[k].astype(F32)
        sx[k] = t.astype(BF16)

        @pl.when(p < NX - 1)
        def _():
            tx_copy(k).start()

        @pl.when(p == NX - 1)
        def _():
            town[...] = t

    acc = dot(gall[0], xall[0], 1, 0)
    for s in range(1, SLOTS):
        acc = acc + dot(gall[s], xall[s], 1, 0)
    qv[...] = norm_vjp(qraw[...], acc * INV_TEMPER).astype(BF16)

    qfull[...] = dot(hq[...], qv[...], 0, 0)

    def core_rows(i, core):
        return pl.ds(pl.multiple_of(i * ROWS + core * HALF, HALF), HALF)

    for i in range(NY):
        qsrc[i] = qfull[core_rows(i, oc), :].astype(BF16)
    qc_cp = push(qsrc, qrc, qc_ss.at[0], qc_rs.at[0], other)

    for k in (1, 3, 2):
        tx_copy(k).wait_recv()
    t = town[...]
    for k in range(NX - 1):
        t = t + rx[k].astype(F32)
    sg[...] = stack(t).astype(BF16)
    tp_cp = [push(sg.at[pg(i)], rg.at[i], tp_ss.at[i], tp_rs.at[i], pp(i)) for i in range(len(plane))]

    qc_cp.wait_recv()
    for i in range(NY):
        q = qfull[core_rows(i, c), :] + qrc[i].astype(F32)
        qsx[:, i] = q.reshape(NX, LINE, DOUT).astype(BF16)
    qx_cp = [
        push(qsx.at[(x + k) % NX], qrx.at[k - 1], qx_ss.at[k - 1], qx_rs.at[k - 1], xp(k))
        for k in (1, 3, 2)
    ]

    for cp in tp_cp:
        cp.wait_recv()
    t = sg[mine].astype(F32)
    for i in range(len(plane)):
        t = t + rg[i].astype(F32)
    t = jnp.concatenate([t[:8], t[8:]], axis=1)
    rgv[mine] = stack(norm_vjp(iraw, t))[0].astype(BF16)
    gp_cp = [push(rgv.at[mine], rgv.at[mine], gp_ss.at[i], gp_rs.at[i], pp(i)) for i in range(len(plane))]

    for cp in qx_cp:
        cp.wait_recv()
    q = qsx[x].astype(F32)
    for k in range(NX - 1):
        q = q + qrx[k].astype(F32)
    qsy[...] = q.astype(BF16)
    qy_cp = [
        push(qsy.at[(y + k) % NY], qry.at[k - 1], qyr_ss.at[k - 1], qyr_rs.at[k - 1], yp(k))
        for k in range(1, NY)
    ]

    for cp in qy_cp:
        cp.wait_recv()
    q = qsy[y].astype(F32)
    for k in range(NY - 1):
        q = q + qry[k].astype(F32)
    qz[z] = q.astype(BF16)
    qz_cp = [
        push(qz.at[z], qz.at[z], qz_ss.at[k - 1], qz_rs.at[k - 1], zp(k)) for k in range(1, NZ)
    ]

    for cp in hy_cp:
        cp.wait_recv()
    for cp in gp_cp:
        cp.wait_recv()
    left, right = unstack(rgv[...].astype(F32))
    raw_grad = jnp.concatenate([left, right], axis=1).astype(BF16)
    aown[...] = dot(hcol[...].reshape(BLOCK, ROWS), raw_grad, 0, 0)
    ac_cp = push(aown.at[core_rows(0, oc)], arc, ac_ss.at[0], ac_rs.at[0], other)

    ac_cp.wait_recv()
    asx[...] = (aown[core_rows(0, c), :] + arc[...]).reshape(NX, LINE, DOUT)
    ax_cp = [
        push(asx.at[(x + k) % NX], arx.at[k - 1], ax_ss.at[k - 1], ax_rs.at[k - 1], xp(k))
        for k in (1, 3, 2)
    ]

    def square_sum(v):
        v = jnp.sum(v * v, axis=0, keepdims=True)
        return v[:, :HALF] + v[:, HALF:]

    def gather(m):
        return [
            push(fin[m].at[y, c, x], fin[m].at[y, c, x], f_ss.at[m, i], f_rs.at[m, i], sp(kx, ky))
            for i, (kx, ky) in enumerate(sheet)
        ]

    for cp in qz_cp:
        cp.wait_recv()
    q = qz[0].astype(F32)
    for k in range(1, NZ):
        q = q + qz[k].astype(F32)
    fin_query[y, c, x] = q.astype(BF16)
    qf_cp = gather(0)

    for cp in ax_cp:
        cp.wait_recv()
    a = asx[x]
    for k in range(NX - 1):
        a = a + arx[k]
    fin_item[y, c, x] = a.astype(BF16)
    af_cp = gather(1)
    nrm[y, x] = square_sum(q) + square_sum(a)
    n_cp = [
        push(nrm.at[y, x], nrm.at[y, x], n_ss.at[i], n_rs.at[i], sp(kx, ky))
        for i, (kx, ky) in enumerate(sheet)
    ]
    fc_cp = []
    for m, cps in ((0, qf_cp), (1, af_cp)):
        for ky in range(NY):
            for cp, (_, k) in zip(cps, sheet):
                if k == ky:
                    cp.wait_recv()
            block = fin[m].at[(y + NY - ky) % NY, c]
            fc_cp.append(push(block, block, fc_ss.at[m, ky], fc_rs.at[m, ky], other))
    for cp in n_cp:
        cp.wait_recv()
    square = jnp.sum(nrm[...].reshape(NX * NY, HALF), axis=0, keepdims=True)
    nsum[0] = square
    ns_cp = push(nsum.at[0], nsum.at[1], ns_ss.at[0], ns_rs.at[0], other)
    ns_cp.wait_recv()
    norm = jnp.sqrt(jnp.sum(square + nsum[1], axis=1, keepdims=True))
    limit = (HID * DOUT / 2) ** 0.5
    factor_ref[...] = jnp.broadcast_to(limit / jnp.maximum(norm, limit), (1, DOUT))
    for cp in fc_cp:
        cp.wait_recv()
    for cp in sent:
        cp.wait_send()
    for k in range(1, NX):
        vx_copy(k).wait_send()
        tx_copy(k).wait_send()
    for k in range(NX):
        vc_copy(k).wait_send()
        tc_copy(k).wait_send()

    @pl.loop(0, CHUNKS)
    def _(ch):
        for k in range(1, NY):
            row_copy(ch, k).wait_send()
        for k in range(1, NZ):
            zrow_copy(ch, k).wait_send()


def local(
    user_features, w_query_in, w_query_out, quo_table, rem_table, w_item_in, w_item_out,
    quo_bucket, rem_bucket, counts, positive,
):
    def vm(*shape, dtype=BF16):
        return pltpu.VMEM(shape, dtype)

    def dma(*shape):
        return [pltpu.SemaphoreType.DMA(shape)] * 2

    anyspace = pl.BlockSpec(memory_space=pl.ANY)
    vmem = pl.BlockSpec(memory_space=pltpu.VMEM)
    smem = pl.BlockSpec(memory_space=pltpu.SMEM)
    scratch = [
        vm(TOK, DIN), vm(DIN, HID), vm(HID, DOUT), vm(4 * SHARD, DIN), vm(DIN, HID), vm(HID, DOUT),
        vm(NY, HALF, dtype=jnp.int32), vm(PLANE - 1, NY, HALF, dtype=jnp.int32), vm(NY, HALF, 4 * SHARD),
        vm(CHUNKS, NY, HALF, WIDE), vm(CHUNKS, NY - 1, HALF, WIDE),
        vm(CHUNKS, NZ, 16, WIDE), vm(CHUNKS, NZ - 1, 16, WIDE), vm(16, HID, dtype=F32),
        vm(TOK, HID), vm(TOK, DOUT, dtype=F32), vm(TOK, DOUT),
        vm(SLOTS, BLOCK, DOUT), vm(PLANE, 16, HALF), vm(NZ, 16, 512), vm(NY, 64, ROWS), vm(NY, 64, ROWS),
        vm(SLOTS, TOK, BLOCK, dtype=F32), vm(TOK, HALF, dtype=F32), vm(TOK, HALF, dtype=F32),
        vm(TOK, HALF, dtype=jnp.int32), vm(TOK, HALF, dtype=F32), vm(SLOTS, TOK, BLOCK),
        vm(NX, BLOCK, DOUT), vm(NX, BLOCK, DOUT), vm(NX, BLOCK, DOUT), vm(NX - 1, BLOCK, DOUT),
        vm(BLOCK, DOUT, dtype=F32), vm(PLANE, 16, HALF), vm(PLANE - 1, 16, HALF),
        vm(PLANE, 16, HALF), vm(HALF, DOUT, dtype=F32), vm(ROWS, DOUT, dtype=F32),
        vm(NX, LINE, DOUT, dtype=F32), vm(NX - 1, LINE, DOUT, dtype=F32),
        vm(HID, DOUT, dtype=F32), vm(NY, HALF, DOUT), vm(NY, HALF, DOUT),
        vm(NX, NY, LINE, DOUT), vm(NX - 1, NY, LINE, DOUT), vm(NY, LINE, DOUT), vm(NY - 1, LINE, DOUT),
        vm(NZ, LINE, DOUT),
        vm(NY, NX, 1, HALF, dtype=F32), vm(2, 1, HALF, dtype=F32), vm(SLOTS, 1, BLOCK, dtype=F32),
        pltpu.SemaphoreType.DMA((7,)),
        *dma(31), *dma(2), *dma(CHUNKS, 3), *dma(CHUNKS, 7),
        *dma(31), *dma(3), *dma(4),
        *dma(7), *dma(3),
        *dma(4), *dma(3), *dma(31),
        *dma(31),
        *dma(1), *dma(3),
        *dma(1), *dma(3), *dma(3), *dma(7),
        *dma(2, 15), *dma(2, 4), *dma(15), *dma(1),
    ]
    losses, grad_query, grad_item, factor = pl.pallas_call(
        kernel,
        out_shape=(
            jax.ShapeDtypeStruct((TOK // HALF, HALF), F32),
            jax.ShapeDtypeStruct((NY, NC, NX, LINE, DOUT), BF16),
            jax.ShapeDtypeStruct((NY, NC, NX, LINE, DOUT), BF16),
            jax.ShapeDtypeStruct((1, DOUT), F32),
        ),
        in_specs=[smem] * 2 + [anyspace] * 7 + [vmem] * 2,
        out_specs=(vmem, vmem, vmem, vmem),
        scratch_shapes=scratch,
        compiler_params=pltpu.CompilerParams(
            collective_id=0, has_side_effects=True, vmem_limit_bytes=56 * 2**20
        ),
        cost_estimate=pl.CostEstimate(flops=6_500_000_000, bytes_accessed=12_000_000, transcendentals=2_100_000),
        name="step",
    )(
        quo_bucket, rem_bucket, user_features, w_query_in, w_query_out, quo_table, rem_table, w_item_in,
        w_item_out, counts.reshape(16, HALF), positive.reshape(TOK // HALF, HALF),
    )
    def scaled(grad):
        return grad.reshape(HID, DOUT).astype(F32) * factor

    return (losses.reshape(TOK), scaled(grad_query), scaled(grad_item))


def solution(mesh):
    in_specs = (
        P(("sec", "dev"), None), P(), P(), P("dev", None), P("dev", None), P(), P(),
        P("dev"), P("dev"), P(), P(("sec", "dev")),
    )
    out_specs = (P(("sec", "dev")), P(), P())
    return jax.shard_map(local, mesh=mesh, in_specs=in_specs, out_specs=out_specs, check_vma=False)
```

time: 1340 us -> 108 us (0.08)
  waiting for transfers between devices: 921 us -> 0 us
  blocking collectives: 325 us -> 0 us
  Pallas kernels: 0 us -> 104 us
  matrix products: 30.3 us -> 0 us
  local copies, waits for them, and re-layouts: 19.5 us -> 0.6 us
  between operations: 16 us -> 0.65 us
    reduce_scatter x2 -> x0, waiting for transfers between devices: 383 us -> none  [the longest x1 306 us: local(): lax.psum_scatter(jnp.einsum('qi,qd->id', logit_gradient, query_embedding_...]
    psum x1 -> x0, waiting for transfers between devices: 264 us -> none  [local(): query_sum, item_sum = lax.psum((query_term, item_term), ('sec', 'dev'))]
    unnamed x1 -> x0, blocking collectives: 258 us -> none
    all_gather x1 -> x0, waiting for transfers between devices: 240 us -> none  [local(): every_item_row = lax.all_gather(block_vectors, 'dev', axis=0, tiled=True)]
    pallas_call x0 -> x1, Pallas kernels: none -> 104 us  [local(): pl.pallas_call(kernel, out_shape=(jax.ShapeDtypeStruct((TOK // HALF, HALF...]
    all_gather x1 -> x0, blocking collectives: 67.1 us -> none  [local(): lax.all_gather(item_embedding_rows, 'sec', axis=0, tiled=True)]
    all_to_all x2 -> x0, waiting for transfers between devices: 34.2 us -> none  [the longest x1 17.7 us: local(): lax.all_to_all(serve(requested(rem_all), rem_table), 'dev', split_axis=0,...]
    dot_general x11 -> x0, matrix products: 30.3 us -> none  [the longest x1 6.26 us: local(): jnp.einsum('qd,id->qi', query_embedding_rows, every_item_row, preferred_e...]
  transfers between devices with their start and end apart: 6 -> 0, of which waited for: 6 -> 0; matrix products, arithmetic and copies ran while one was open for 1% -> 0% of each run, Pallas kernels for 0% -> 0%
where the time goes in v2:
time: 108 us
  Pallas kernels  104 us (96%)
  other arithmetic  2.69 us (2%)
    pallas_call x1, Pallas kernels, local(): pl.pallas_call(kernel, out_shape=(jax.ShapeDtypeStruct((TOK // HALF, HALF...  104 us
    mul x1, other arithmetic, scaled(): return grad.reshape(HID, DOUT).astype(F32) * factor  2.69 us

profile of v2, /device:TPU:1, one launch (start us, length us, event | category | flops | bytes accessed | tf_op | source)
XLA Modules:
  0.0 108.3 jit_solution(3143831722281424713)
XLA Ops:
  0.6 104.3 %step.1 = (f32[8,128]{1,0:T(8,128)}, bf16[4,2,4,32,256]{4,3,2,1,0:T(8,128)(2,1)}, bf16[4,2,4,32,256]{4,3,2,1,0:T(8,128)(2,1)}, f32[1,256]{1,0:T(1,128)}) custom-call(s32[32]{0:T(128)} %quo_idx.1, s32[32]{0:T(128)} %rem_idx.1, bf16[1024,1024]{1,0:T(8,128)(2,1)} %feat_hbm.1, bf16[1024,1024]{1,0:T(8,128)(2,1)} %wqi_hbm.1, bf16[1024,256]{1,0:T(8,128)(2,1)} %wqo_hbm.1, ...), custom_call_target="tpu_custom_call" | custom-call | flops 6499999744 | bytes 12000000 | tf_op jit(solution)/shard_map/step/pallas_call | solution.py:567
  105.0 0.0 copy-start
  105.0 2.7 %convert_multiply_fusion = (f32[1024,256]{1,0:T(8,128)}, f32[1024,256]{1,0:T(8,128)}) fusion(bf16[4,2,4,32,256]{4,3,2,1,0:T(8,128)(2,1)} %get-tuple-element.10, f32[256]{0:T(256)} %bitcast.11, bf16[4,2,4,32,256]{4,3,2,1,0:T(8,128)(2,1)} %get-tuple-element.8), kind=kLoop, calls=%fused_computation | loop fusion | flops 1048576 | bytes 3146752 | tf_op jit(solution)/shard_map/mul | solution.py:588
  107.7 0.0 copy-done
  107.7 0.6 copy.15
Async XLA Ops:
  105.0 2.7 %copy-start = (f32[8,128]{1,0:T(8,128)S(1)}, f32[8,128]{1,0:T(8,128)}, u32[]{:S(2)}) copy-start(f32[8,128]{1,0:T(8,128)} %get-tuple-element.7) | copy-start | bytes 12292

commit v3 on v2

--- a/solution.py
+++ b/solution.py
@@ -21,6 +21,7 @@
 SHARD = 128
 TROWS = 8192
 CHUNKS = 4
+ORDER = (0, 1, 2, 3)
 WIDE = DIN // CHUNKS
 TILE = 256
 HALF = 128
@@ -77,7 +78,7 @@
     tc_ss, tc_rs, tx_ss, tx_rs, tp_ss, tp_rs,
     gp_ss, gp_rs,
     ac_ss, ac_rs, ax_ss, ax_rs,
-    qc_ss, qc_rs, qx_ss, qx_rs, qyr_ss, qyr_rs, qz_ss, qz_rs,
+    qc_ss, qc_rs, qx_ss, qx_rs, qy_ss, qy_rs, qz_ss, qz_rs,
     f_ss, f_rs, fc_ss, fc_rs, n_ss, n_rs, ns_ss, ns_rs,
 ):
     sec = lax.axis_index("sec")
@@ -132,6 +133,17 @@
         sent.append(cp)
         return cp
 
+    def landed(region, rs):
+        copy(region, region, rs, rs, other).wait_recv()
+
+    def left_here(region, ss):
+        sent.append(copy(region, region, ss, ss, other))
+
+    def flush():
+        for cp in sent:
+            cp.wait_send()
+        sent.clear()
+
     barrier = pltpu.get_barrier_semaphore()
     for i in range(len(plane)):
         pl.semaphore_signal(barrier, inc=1, device_id=pp(i), device_id_type=MESH)
@@ -143,20 +155,17 @@
             pl.semaphore_signal(barrier, inc=1, device_id=sp(kx, ky), device_id_type=MESH)
 
     loads = []
-    for i, (src, dst) in enumerate(
-        [
-            (quo_hbm, tab.at[pl.ds(0, SHARD)]),
-            (rem_hbm, tab.at[pl.ds(2 * SHARD, SHARD)]),
-            (feat_hbm, feat),
-            (wqi_hbm, wqi),
-            (wqo_hbm, wqo),
-            (wii_hbm, wii),
-            (wio_hbm, wio),
-        ]
-    ):
-        cp = pltpu.make_async_copy(src, dst, load_sem.at[i])
+
+    def load(src, dst):
+        cp = pltpu.make_async_copy(src, dst, load_sem.at[len(loads)])
         cp.start()
         loads.append(cp)
+
+    for ch in range(CHUNKS):
+        load(quo_hbm.at[:, ch * WIDE : (ch + 1) * WIDE], tab.at[ch, pl.ds(0, SHARD)])
+        load(rem_hbm.at[:, ch * WIDE : (ch + 1) * WIDE], tab.at[ch, pl.ds(2 * SHARD, SHARD)])
+    for src, dst in ((feat_hbm, feat), (wqi_hbm, wqi), (wqo_hbm, wqo), (wii_hbm, wii), (wio_hbm, wio)):
+        load(src, dst)
 
     lane = lax.broadcasted_iota(jnp.int32, (NY, HALF), 1) - z * 2 * QUARTER
     lane = jnp.where(lax.broadcasted_iota(jnp.int32, (NY, HALF), 0) == y, lane, -1)
@@ -165,16 +174,28 @@
         asked = jnp.where(lane == j, quo_idx[sec * QUARTER + j], asked)
         asked = jnp.where(lane == QUARTER + j, rem_idx[sec * QUARTER + j] + TROWS, asked)
     idx_out[...] = asked
-    loads[0].wait()
-    loads[1].wait()
+    for i in range(2 * CHUNKS):
+        loads[i].wait()
     pl.semaphore_wait(barrier, greeted)
 
-    idx_cp = [
-        push(idx_out, idx_recv.at[i], idx_ss.at[i], idx_rs.at[i], pp(i)) for i in range(len(plane))
-    ]
+    for i in range(len(plane)):
+        copy(idx_out, idx_recv.at[i], idx_ss.at[0], idx_rs.at[0], pp(i)).start()
+    left_here(idx_recv, idx_ss.at[0])
     own_rows = pl.ds(pl.multiple_of(c * 2 * SHARD, SHARD), SHARD)
     their_rows = pl.ds(pl.multiple_of(c * 2 * SHARD + SHARD, SHARD), SHARD)
-    tab_cp = push(tab.at[own_rows], tab.at[their_rows], tab_ss.at[0], tab_rs.at[0], partner)
+
+    def tab_copy(ch):
+        return copy(
+            tab.at[ch, own_rows], tab.at[ch, their_rows], tab_ss.at[0, ch], tab_rs.at[0, ch], partner
+        )
+
+    def tab_core_copy(ch):
+        return copy(
+            tab.at[ch, their_rows], tab.at[ch, their_rows], tab_ss.at[1, ch], tab_rs.at[1, ch], other
+        )
+
+    for ch in ORDER:
+        tab_copy(ch).start()
 
     pos = pos_in[...]
     place = ((pos // 16) % 2) * 1024 + ((pos // 32) % 2) * 512 + ((pos // 8) % 2) * 256
@@ -197,15 +218,14 @@
         wide = dot(high, pick, 1, 0) * 8.0 + dot(low, pick, 1, 0)
         lc_ref[s] = jnp.log(jnp.sum(jnp.where(keep, wide, 0.0), axis=0, keepdims=True)) * LOG2E
 
-    loads[2].wait()
-    loads[3].wait()
+    loads[2 * CHUNKS].wait()
+    loads[2 * CHUNKS + 1].wait()
 
     hq[...] = jnp.maximum(dot(feat[...], wqi[...], 1, 0), 0.0).astype(BF16)
 
-    tab_cp.wait_recv()
-    tabc_cp = push(tab.at[their_rows], tab.at[their_rows], tab_ss.at[1], tab_rs.at[1], other)
-    for cp in idx_cp:
-        cp.wait_recv()
+    tab_copy(ORDER[0]).wait_recv()
+    tab_core_copy(ORDER[0]).start()
+    landed(idx_recv, idx_rs.at[0])
     total = idx_out[...]
     for i in range(len(plane)):
         total = total + idx_recv[i]
@@ -216,20 +236,24 @@
     row_id = line % SHARD + owner * SHARD + (which // 2) * TROWS
     for i in range(NY):
         sel[i] = (row_id == total[:, i : i + 1]).astype(F32).astype(BF16)
-    tabc_cp.wait_recv()
 
     def row_copy(ch, k):
-        return copy(srow.at[ch, k], rrow.at[ch, k - 1], ry_ss.at[ch, k - 1], ry_rs.at[ch, k - 1], yp(k))
-
-    @pl.loop(0, CHUNKS)
-    def _(ch):
-        cols = pl.ds(pl.multiple_of(ch * WIDE, WIDE), WIDE)
+        return copy(srow.at[ch, k], rrow.at[ch, k - 1], ry_ss.at[ch], ry_rs.at[ch], yp(k))
+
+    for i, ch in enumerate(ORDER):
+        if i < CHUNKS - 1:
+            tab_copy(ORDER[i + 1]).wait_recv()
+            tab_core_copy(ORDER[i + 1]).start()
+        tab_core_copy(ch).wait_recv()
         for k in (1, 3, 2, 0):
-            srow[ch, k] = dot(sel[(y + k) % NY], tab[:, cols], 1, 0).astype(BF16)
+            srow[ch, k] = dot(sel[(y + k) % NY], tab[ch], 1, 0).astype(BF16)
             if k:
                 row_copy(ch, k).start()
-
-    loads[4].wait()
+        left_here(rrow.at[ch], ry_ss.at[ch])
+        sent.append(tab_copy(ch))
+        sent.append(tab_core_copy(ch))
+
+    loads[2 * CHUNKS + 2].wait()
 
     raw = dot(hq[...], wqo[...], 1, 0)
     qraw[...] = raw
@@ -237,50 +261,48 @@
 
     def zrow_copy(ch, k):
         return copy(
-            zrow.at[ch, (z + k) % NZ], rzrow.at[ch, k - 1], rz_ss.at[ch, k - 1], rz_rs.at[ch, k - 1], zp(k)
+            zrow.at[ch, (z + k) % NZ], rzrow.at[ch, k - 1], rz_ss.at[ch], rz_rs.at[ch], zp(k)
         )
 
-    @pl.loop(0, CHUNKS)
-    def _(ch):
-        for k in (1, 3, 2):
-            row_copy(ch, k).wait_recv()
+    for ch in ORDER:
+        landed(rrow.at[ch], ry_rs.at[ch])
         s = srow[ch, 0].astype(F32)
         for k in range(NY - 1):
             s = s + rrow[ch, k].astype(F32)
         zrow[ch] = s.astype(BF16).reshape(NZ, 16, WIDE)
         for k in range(1, NZ):
             zrow_copy(ch, k).start()
-
-    loads[5].wait()
-    loads[6].wait()
+    flush()
+    for ch in ORDER:
+        left_here(rzrow.at[ch], rz_ss.at[ch])
+
+    loads[2 * CHUNKS + 3].wait()
+    loads[2 * CHUNKS + 4].wait()
     pre[...] = jnp.zeros_like(pre)
 
-    @pl.loop(0, CHUNKS)
-    def _(ch):
-        for k in range(1, NZ):
-            zrow_copy(ch, k).wait_recv()
+    for ch in ORDER:
+        landed(rzrow.at[ch], rz_rs.at[ch])
         s = zrow[ch, z].astype(F32)
         for k in range(NZ - 1):
             s = s + rzrow[ch, k].astype(F32)
         emb = s[:8] * s[8:]
         emb = jnp.concatenate([emb, emb], axis=0).astype(BF16)
-        rows = pl.ds(pl.multiple_of(ch * WIDE, WIDE), WIDE)
-        pre[...] += dot(emb, wii[rows, :], 1, 0)
+        pre[...] += dot(emb, wii[ch * WIDE : (ch + 1) * WIDE, :], 1, 0)
 
     hid = jnp.maximum(pre[...], 0.0).astype(BF16)
     iraw = dot(hid, wio[...], 1, 0)[:8]
     ivec = iraw * norm_scale(iraw) * (DOUT**-0.5)
     gv[mine] = stack(ivec)[0].astype(BF16)
 
-    v_cp = [
-        push(gv.at[mine], gv.at[mine], vp_ss.at[i], vp_rs.at[i], pp(i)) for i in range(len(plane))
-    ]
+    for i in range(len(plane)):
+        copy(gv.at[mine], gv.at[mine], vp_ss.at[0], vp_rs.at[0], pp(i)).start()
+    flush()
+    left_here(gv.at[pl.ds(0, PLANE - 1)], vp_ss.at[0])
     hid8 = hid.astype(F32)[:8]
     hz[z] = jnp.concatenate([hid8[:, :512], hid8[:, 512:]], axis=0).astype(BF16)
     esum[...] = jnp.zeros_like(esum)
     psum[...] = jnp.zeros_like(psum)
-    for cp in v_cp:
-        cp.wait_recv()
+    landed(gv.at[pl.ds(0, PLANE - 1)], vp_rs.at[0])
     left, right = unstack(gv[...].astype(F32))
     xall[slot, :, :HALF] = left.astype(BF16)
     xall[slot, :, HALF:] = right.astype(BF16)
@@ -290,9 +312,9 @@
 
     for k in (1, 3, 2):
         vx_copy(k).start()
-    hz_cp = [
-        push(hz.at[z], hz.at[z], hz_ss.at[k - 1], hz_rs.at[k - 1], zp(k)) for k in range(1, NZ)
-    ]
+    for k in range(1, NZ):
+        copy(hz.at[z], hz.at[z], hz_ss.at[0], hz_rs.at[0], zp(k)).start()
+    left_here(hz.at[pl.ds(0, NZ - 1)], hz_ss.at[0])
 
     def first_pass(s):
         logit = dot(qv[...], xall[s], 1, 1) * (INV_TEMPER * LOG2E) - lc_ref[s]
@@ -321,18 +343,16 @@
         vc_copy(p).wait_recv()
         first_pass(s + oc)
 
-    for cp in hz_cp:
-        cp.wait_recv()
+    landed(hz.at[pl.ds(0, NZ - 1)], hz_rs.at[0])
     hv = hz[...].astype(F32)
     hv = jnp.concatenate([hv[:, :8, :].reshape(64, 512), hv[:, 8:, :].reshape(64, 512)], axis=1)
     hv = hv.astype(BF16)
     for i in range(NY):
         hsrc[i] = hv[:, i * ROWS : (i + 1) * ROWS]
     hcol[y] = hsrc[y]
-    hy_cp = [
-        push(hsrc.at[(y + k) % NY], hcol.at[y], hy_ss.at[k - 1], hy_rs.at[k - 1], yp(k))
-        for k in range(1, NY)
-    ]
+    for k in range(1, NY):
+        copy(hsrc.at[(y + k) % NY], hcol.at[y], hy_ss.at[0], hy_rs.at[0], yp(k)).start()
+    left_here(hcol.at[pl.ds(0, NY - 1)], hy_ss.at[0])
     sums = jnp.sum(esum[...], axis=1, keepdims=True)
     picked = jnp.sum(psum[...], axis=1, keepdims=True)
     invb[...] = jnp.broadcast_to(1.0 / sums, (TOK, HALF))
@@ -358,7 +378,7 @@
         return copy(tsrc.at[k], rc.at[k], tc_ss.at[k], tc_rs.at[k], other)
 
     def tx_copy(k):
-        return copy(sx.at[k], rx.at[k - 1], tx_ss.at[k - 1], tx_rs.at[k - 1], xp(k))
+        return copy(sx.at[k], rx.at[k - 1], tx_ss.at[0], tx_rs.at[0], xp(k))
 
     @pl.loop(0, NX)
     def _(p):
@@ -395,57 +415,62 @@
         qsrc[i] = qfull[core_rows(i, oc), :].astype(BF16)
     qc_cp = push(qsrc, qrc, qc_ss.at[0], qc_rs.at[0], other)
 
-    for k in (1, 3, 2):
-        tx_copy(k).wait_recv()
+    flush()
+    for k in range(1, NX):
+        sent.append(vx_copy(k))
+    for k in range(NX):
+        sent.append(vc_copy(k))
+        sent.append(tc_copy(k))
+    left_here(rx, tx_ss.at[0])
+    landed(rx, tx_rs.at[0])
     t = town[...]
     for k in range(NX - 1):
         t = t + rx[k].astype(F32)
     sg[...] = stack(t).astype(BF16)
-    tp_cp = [push(sg.at[pg(i)], rg.at[i], tp_ss.at[i], tp_rs.at[i], pp(i)) for i in range(len(plane))]
+    for i in range(len(plane)):
+        copy(sg.at[pg(i)], rg.at[i], tp_ss.at[0], tp_rs.at[0], pp(i)).start()
 
     qc_cp.wait_recv()
     for i in range(NY):
         q = qfull[core_rows(i, c), :] + qrc[i].astype(F32)
         qsx[:, i] = q.reshape(NX, LINE, DOUT).astype(BF16)
-    qx_cp = [
-        push(qsx.at[(x + k) % NX], qrx.at[k - 1], qx_ss.at[k - 1], qx_rs.at[k - 1], xp(k))
-        for k in (1, 3, 2)
-    ]
-
-    for cp in tp_cp:
-        cp.wait_recv()
+    for k in (1, 3, 2):
+        copy(qsx.at[(x + k) % NX], qrx.at[k - 1], qx_ss.at[0], qx_rs.at[0], xp(k)).start()
+    flush()
+    left_here(rg, tp_ss.at[0])
+    left_here(qrx, qx_ss.at[0])
+
+    landed(rg, tp_rs.at[0])
     t = sg[mine].astype(F32)
     for i in range(len(plane)):
         t = t + rg[i].astype(F32)
     t = jnp.concatenate([t[:8], t[8:]], axis=1)
     rgv[mine] = stack(norm_vjp(iraw, t))[0].astype(BF16)
-    gp_cp = [push(rgv.at[mine], rgv.at[mine], gp_ss.at[i], gp_rs.at[i], pp(i)) for i in range(len(plane))]
-
-    for cp in qx_cp:
-        cp.wait_recv()
+    for i in range(len(plane)):
+        copy(rgv.at[mine], rgv.at[mine], gp_ss.at[0], gp_rs.at[0], pp(i)).start()
+
+    landed(qrx, qx_rs.at[0])
     q = qsx[x].astype(F32)
     for k in range(NX - 1):
         q = q + qrx[k].astype(F32)
     qsy[...] = q.astype(BF16)
-    qy_cp = [
-        push(qsy.at[(y + k) % NY], qry.at[k - 1], qyr_ss.at[k - 1], qyr_rs.at[k - 1], yp(k))
-        for k in range(1, NY)
-    ]
-
-    for cp in qy_cp:
-        cp.wait_recv()
+    for k in range(1, NY):
+        copy(qsy.at[(y + k) % NY], qry.at[k - 1], qy_ss.at[0], qy_rs.at[0], yp(k)).start()
+    flush()
+    left_here(rgv.at[pl.ds(0, PLANE - 1)], gp_ss.at[0])
+    left_here(qry, qy_ss.at[0])
+
+    landed(qry, qy_rs.at[0])
     q = qsy[y].astype(F32)
     for k in range(NY - 1):
         q = q + qry[k].astype(F32)
     qz[z] = q.astype(BF16)
-    qz_cp = [
-        push(qz.at[z], qz.at[z], qz_ss.at[k - 1], qz_rs.at[k - 1], zp(k)) for k in range(1, NZ)
-    ]
-
-    for cp in hy_cp:
-        cp.wait_recv()
-    for cp in gp_cp:
-        cp.wait_recv()
+    for k in range(1, NZ):
+        copy(qz.at[z], qz.at[z], qz_ss.at[0], qz_rs.at[0], zp(k)).start()
+    left_here(qz.at[pl.ds(0, NZ - 1)], qz_ss.at[0])
+
+    landed(hcol.at[pl.ds(0, NY - 1)], hy_rs.at[0])
+    landed(rgv.at[pl.ds(0, PLANE - 1)], gp_rs.at[0])
     left, right = unstack(rgv[...].astype(F32))
     raw_grad = jnp.concatenate([left, right], axis=1).astype(BF16)
     aown[...] = dot(hcol[...].reshape(BLOCK, ROWS), raw_grad, 0, 0)
@@ -453,51 +478,56 @@
 
     ac_cp.wait_recv()
     asx[...] = (aown[core_rows(0, c), :] + arc[...]).reshape(NX, LINE, DOUT)
-    ax_cp = [
-        push(asx.at[(x + k) % NX], arx.at[k - 1], ax_ss.at[k - 1], ax_rs.at[k - 1], xp(k))
-        for k in (1, 3, 2)
-    ]
+    for k in (1, 3, 2):
+        copy(asx.at[(x + k) % NX], arx.at[k - 1], ax_ss.at[0], ax_rs.at[0], xp(k)).start()
+    flush()
+    left_here(arx, ax_ss.at[0])
 
     def square_sum(v):
         v = jnp.sum(v * v, axis=0, keepdims=True)
         return v[:, :HALF] + v[:, HALF:]
 
+    def group(ref, ky, lead):
+        return ref.at[lead + (pl.ds(0, NX - 1),)] if ky == 0 else ref.at[lead]
+
     def gather(m):
-        return [
-            push(fin[m].at[y, c, x], fin[m].at[y, c, x], f_ss.at[m, i], f_rs.at[m, i], sp(kx, ky))
-            for i, (kx, ky) in enumerate(sheet)
-        ]
-
-    for cp in qz_cp:
-        cp.wait_recv()
+        for kx, ky in sheet:
+            copy(
+                fin[m].at[y, c, x], fin[m].at[y, c, x], f_ss.at[m, ky], f_rs.at[m, ky], sp(kx, ky)
+            ).start()
+        for ky in range(NY):
+            left_here(group(fin[m], ky, (0, 0)), f_ss.at[m, ky])
+
+    def gather_core(m):
+        for ky in range(NY):
+            landed(group(fin[m], ky, (0, 0)), f_rs.at[m, ky])
+            block = fin[m].at[(y + NY - ky) % NY, c]
+            fc_cp.append(push(block, block, fc_ss.at[m, ky], fc_rs.at[m, ky], other))
+
+    fc_cp = []
+
+    landed(qz.at[pl.ds(0, NZ - 1)], qz_rs.at[0])
     q = qz[0].astype(F32)
     for k in range(1, NZ):
         q = q + qz[k].astype(F32)
     fin_query[y, c, x] = q.astype(BF16)
-    qf_cp = gather(0)
-
-    for cp in ax_cp:
-        cp.wait_recv()
+    gather(0)
+
+    landed(arx, ax_rs.at[0])
     a = asx[x]
     for k in range(NX - 1):
         a = a + arx[k]
     fin_item[y, c, x] = a.astype(BF16)
-    af_cp = gather(1)
+    gather(1)
     nrm[y, x] = square_sum(q) + square_sum(a)
-    n_cp = [
-        push(nrm.at[y, x], nrm.at[y, x], n_ss.at[i], n_rs.at[i], sp(kx, ky))
-        for i, (kx, ky) in enumerate(sheet)
-    ]
-    fc_cp = []
-    for m, cps in ((0, qf_cp), (1, af_cp)):
-        for ky in range(NY):
-            for cp, (_, k) in zip(cps, sheet):
-                if k == ky:
-                    cp.wait_recv()
-            block = fin[m].at[(y + NY - ky) % NY, c]
-            fc_cp.append(push(block, block, fc_ss.at[m, ky], fc_rs.at[m, ky], other))
-    for cp in n_cp:
-        cp.wait_recv()
+    for kx, ky in sheet:
+        copy(nrm.at[y, x], nrm.at[y, x], n_ss.at[ky], n_rs.at[ky], sp(kx, ky)).start()
+    gather_core(0)
+    flush()
+    gather_core(1)
+    for ky in range(NY):
+        left_here(group(nrm, ky, (0,)), n_ss.at[ky])
+        landed(group(nrm, ky, (0,)), n_rs.at[ky])
     square = jnp.sum(nrm[...].reshape(NX * NY, HALF), axis=0, keepdims=True)
     nsum[0] = square
     ns_cp = push(nsum.at[0], nsum.at[1], ns_ss.at[0], ns_rs.at[0], other)
@@ -507,21 +537,7 @@
     factor_ref[...] = jnp.broadcast_to(limit / jnp.maximum(norm, limit), (1, DOUT))
     for cp in fc_cp:
         cp.wait_recv()
-    for cp in sent:
-        cp.wait_send()
-    for k in range(1, NX):
-        vx_copy(k).wait_send()
-        tx_copy(k).wait_send()
-    for k in range(NX):
-        vc_copy(k).wait_send()
-        tc_copy(k).wait_send()
-
-    @pl.loop(0, CHUNKS)
-    def _(ch):
-        for k in range(1, NY):
-            row_copy(ch, k).wait_send()
-        for k in range(1, NZ):
-            zrow_copy(ch, k).wait_send()
+    flush()
 
 
 def local(
@@ -538,7 +554,7 @@
     vmem = pl.BlockSpec(memory_space=pltpu.VMEM)
     smem = pl.BlockSpec(memory_space=pltpu.SMEM)
     scratch = [
-        vm(TOK, DIN), vm(DIN, HID), vm(HID, DOUT), vm(4 * SHARD, DIN), vm(DIN, HID), vm(HID, DOUT),
+        vm(TOK, DIN), vm(DIN, HID), vm(HID, DOUT), vm(CHUNKS, 4 * SHARD, WIDE), vm(DIN, HID), vm(HID, DOUT),
         vm(NY, HALF, dtype=jnp.int32), vm(PLANE - 1, NY, HALF, dtype=jnp.int32), vm(NY, HALF, 4 * SHARD),
         vm(CHUNKS, NY, HALF, WIDE), vm(CHUNKS, NY - 1, HALF, WIDE),
         vm(CHUNKS, NZ, 16, WIDE), vm(CHUNKS, NZ - 1, 16, WIDE), vm(16, HID, dtype=F32),
@@ -554,15 +570,15 @@
         vm(NX, NY, LINE, DOUT), vm(NX - 1, NY, LINE, DOUT), vm(NY, LINE, DOUT), vm(NY - 1, LINE, DOUT),
         vm(NZ, LINE, DOUT),
         vm(NY, NX, 1, HALF, dtype=F32), vm(2, 1, HALF, dtype=F32), vm(SLOTS, 1, BLOCK, dtype=F32),
-        pltpu.SemaphoreType.DMA((7,)),
-        *dma(31), *dma(2), *dma(CHUNKS, 3), *dma(CHUNKS, 7),
-        *dma(31), *dma(3), *dma(4),
-        *dma(7), *dma(3),
-        *dma(4), *dma(3), *dma(31),
-        *dma(31),
-        *dma(1), *dma(3),
-        *dma(1), *dma(3), *dma(3), *dma(7),
-        *dma(2, 15), *dma(2, 4), *dma(15), *dma(1),
+        pltpu.SemaphoreType.DMA((2 * CHUNKS + 5,)),
+        *dma(1), *dma(2, CHUNKS), *dma(CHUNKS), *dma(CHUNKS),
+        *dma(1), *dma(3), *dma(4),
+        *dma(1), *dma(1),
+        *dma(4), *dma(1), *dma(1),
+        *dma(1),
+        *dma(1), *dma(1),
+        *dma(1), *dma(1), *dma(1), *dma(1),
+        *dma(2, 4), *dma(2, 4), *dma(4), *dma(1),
     ]
     losses, grad_query, grad_item, factor = pl.pallas_call(
         kernel,

time: 108 us -> 102 us (0.944)
  Pallas kernels: 104 us -> 98.3 us
    pallas_call x1, Pallas kernels: 104 us -> 98.3 us  [local(): pl.pallas_call(kernel, out_shape=(jax.ShapeDtypeStruct((TOK // HALF, HALF...]
where the time goes in v3:
time: 102 us
  Pallas kernels  98.3 us (96%)
  other arithmetic  2.69 us (3%)
    pallas_call x1, Pallas kernels, local(): pl.pallas_call(kernel, out_shape=(jax.ShapeDtypeStruct((TOK // HALF, HALF...  98.3 us
    mul x1, other arithmetic, scaled(): return grad.reshape(HID, DOUT).astype(F32) * factor  2.69 us

profile of v3, /device:TPU:1, one launch (start us, length us, event | category | flops | bytes accessed | tf_op | source)
XLA Modules:
  0.0 102.2 jit_solution(3359932085113918886)
XLA Ops:
  0.6 98.3 %step.1 = (f32[8,128]{1,0:T(8,128)}, bf16[4,2,4,32,256]{4,3,2,1,0:T(8,128)(2,1)}, bf16[4,2,4,32,256]{4,3,2,1,0:T(8,128)(2,1)}, f32[1,256]{1,0:T(1,128)}) custom-call(s32[32]{0:T(128)} %quo_idx.1, s32[32]{0:T(128)} %rem_idx.1, bf16[1024,1024]{1,0:T(8,128)(2,1)} %feat_hbm.1, bf16[1024,1024]{1,0:T(8,128)(2,1)} %wqi_hbm.1, bf16[1024,256]{1,0:T(8,128)(2,1)} %wqo_hbm.1, ...), custom_call_target="tpu_custom_call" | custom-call | flops 6499999744 | bytes 12000000 | tf_op jit(solution)/shard_map/step/pallas_call | solution.py:583
  98.9 0.0 copy-start
  99.0 2.7 %convert_multiply_fusion = (f32[1024,256]{1,0:T(8,128)}, f32[1024,256]{1,0:T(8,128)}) fusion(bf16[4,2,4,32,256]{4,3,2,1,0:T(8,128)(2,1)} %get-tuple-element.10, f32[256]{0:T(256)} %bitcast.11, bf16[4,2,4,32,256]{4,3,2,1,0:T(8,128)(2,1)} %get-tuple-element.8), kind=kLoop, calls=%fused_computation | loop fusion | flops 1048576 | bytes 3146752 | tf_op jit(solution)/shard_map/mul | solution.py:604
  101.6 0.0 copy-done
  101.6 0.6 copy.15
Async XLA Ops:
  98.9 2.7 %copy-start = (f32[8,128]{1,0:T(8,128)S(1)}, f32[8,128]{1,0:T(8,128)}, u32[]{:S(2)}) copy-start(f32[8,128]{1,0:T(8,128)} %get-tuple-element.7) | copy-start | bytes 12292

commit v4 on v3

--- a/solution.py
+++ b/solution.py
@@ -21,7 +21,15 @@
 SHARD = 128
 TROWS = 8192
 CHUNKS = 4
-ORDER = (0, 1, 2, 3)
+ZFIRST = 3
+ORDER = (0, ZFIRST, 1, 2)
+
+
+def hops(k, n):
+    return min(k, n - k)
+
+
+Z_FAR = sorted(range(1, NZ), key=lambda k: -hops(k, NZ))
 WIDE = DIN // CHUNKS
 TILE = 256
 HALF = 128
@@ -57,22 +65,21 @@
     return left, right
 
 
-def gray(p):
-    return p + jnp.where(p == 2, 1, 0) - jnp.where(p == 3, 1, 0)
+GRAY = (0, 1, 3, 2)
 
 
 def kernel(
     quo_idx, rem_idx, feat_hbm, wqi_hbm, wqo_hbm, quo_hbm, rem_hbm, wii_hbm, wio_hbm, counts_in, pos_in,
     loss_ref, fin_query, fin_item, factor_ref,
     feat, wqi, wqo, tab, wii, wio,
-    idx_out, idx_recv, sel, srow, rrow, zrow, rzrow, pre,
+    idx_out, idx_recv, sel, srow, rrow, zrow, rzrow, srz, rrz, sry, rry, pre,
     hq, qraw, qv, xall, gv, hz, hsrc, hcol,
     est, esum, psum, posb, invb, gall, tsrc, rc, sx, rx, town, sg, rg,
     rgv, arc, aown, asx, arx,
     qfull, qsrc, qrc, qsx, qrx, qsy, qry, qz,
     nrm, nsum, lc_ref,
     load_sem,
-    idx_ss, idx_rs, tab_ss, tab_rs, ry_ss, ry_rs, rz_ss, rz_rs,
+    idx_ss, idx_rs, tab_ss, tab_rs, ry_ss, ry_rs, rz_ss, rz_rs, rf_ss, rf_rs, rl_ss, rl_rs,
     vp_ss, vp_rs, vx_ss, vx_rs, vc_ss, vc_rs,
     hz_ss, hz_rs, hy_ss, hy_rs,
     tc_ss, tc_rs, tx_ss, tx_rs, tp_ss, tp_rs,
@@ -104,7 +111,9 @@
 
     other = at(x, oc, y, z)
     plane = [(ky, kz) for ky in range(NY) for kz in range(NZ) if ky or kz]
+    plane.sort(key=lambda p: -hops(p[0], NY) - hops(p[1], NZ))
     sheet = [(kx, ky) for ky in range(NY) for kx in range(NX) if kx or ky]
+    sheet.sort(key=lambda p: -hops(p[0], NX) - hops(p[1], NY))
 
     def sp(kx, ky):
         return at((x + kx) % NX, c, (y + ky) % NY, z)
@@ -245,11 +254,19 @@
             tab_copy(ORDER[i + 1]).wait_recv()
             tab_core_copy(ORDER[i + 1]).start()
         tab_core_copy(ch).wait_recv()
-        for k in (1, 3, 2, 0):
-            srow[ch, k] = dot(sel[(y + k) % NY], tab[ch], 1, 0).astype(BF16)
-            if k:
-                row_copy(ch, k).start()
-        left_here(rrow.at[ch], ry_ss.at[ch])
+        if ch == ZFIRST:
+            for i in range(NY):
+                got = dot(sel[i], tab[ch], 1, 0).astype(BF16)
+                srz[:, i * 16 : (i + 1) * 16, :] = got.reshape(NZ, 16, WIDE)
+            for k in Z_FAR:
+                copy(srz.at[(z + k) % NZ], rrz.at[k - 1], rf_ss.at[0], rf_rs.at[0], zp(k)).start()
+            left_here(rrz, rf_ss.at[0])
+        else:
+            for k in (2, 1, 3, 0):
+                srow[ch, k] = dot(sel[(y + k) % NY], tab[ch], 1, 0).astype(BF16)
+                if k:
+                    row_copy(ch, k).start()
+            left_here(rrow.at[ch], ry_ss.at[ch])
         sent.append(tab_copy(ch))
         sent.append(tab_core_copy(ch))
 
@@ -264,27 +281,43 @@
             zrow.at[ch, (z + k) % NZ], rzrow.at[ch, k - 1], rz_ss.at[ch], rz_rs.at[ch], zp(k)
         )
 
-    for ch in ORDER:
+    def along_z(ch):
         landed(rrow.at[ch], ry_rs.at[ch])
         s = srow[ch, 0].astype(F32)
         for k in range(NY - 1):
             s = s + rrow[ch, k].astype(F32)
         zrow[ch] = s.astype(BF16).reshape(NZ, 16, WIDE)
-        for k in range(1, NZ):
+        for k in Z_FAR:
             zrow_copy(ch, k).start()
-    flush()
-    for ch in ORDER:
         left_here(rzrow.at[ch], rz_ss.at[ch])
+
+    along_z(0)
+    along_z(1)
+    landed(rrz, rf_rs.at[0])
+    s = srz[z].astype(F32)
+    for k in range(NZ - 1):
+        s = s + rrz[k].astype(F32)
+    sry[...] = s.astype(BF16).reshape(NY, 16, WIDE)
+    for k in (2, 1, 3):
+        copy(sry.at[(y + k) % NY], rry.at[k - 1], rl_ss.at[0], rl_rs.at[0], yp(k)).start()
+    left_here(rry, rl_ss.at[0])
+    along_z(2)
 
     loads[2 * CHUNKS + 3].wait()
     loads[2 * CHUNKS + 4].wait()
     pre[...] = jnp.zeros_like(pre)
 
-    for ch in ORDER:
-        landed(rzrow.at[ch], rz_rs.at[ch])
-        s = zrow[ch, z].astype(F32)
-        for k in range(NZ - 1):
-            s = s + rzrow[ch, k].astype(F32)
+    for ch in (0, 1, ZFIRST, 2):
+        if ch == ZFIRST:
+            landed(rry, rl_rs.at[0])
+            s = sry[y].astype(F32)
+            for k in range(NY - 1):
+                s = s + rry[k].astype(F32)
+        else:
+            landed(rzrow.at[ch], rz_rs.at[ch])
+            s = zrow[ch, z].astype(F32)
+            for k in range(NZ - 1):
+                s = s + rzrow[ch, k].astype(F32)
         emb = s[:8] * s[8:]
         emb = jnp.concatenate([emb, emb], axis=0).astype(BF16)
         pre[...] += dot(emb, wii[ch * WIDE : (ch + 1) * WIDE, :], 1, 0)
@@ -312,7 +345,7 @@
 
     for k in (1, 3, 2):
         vx_copy(k).start()
-    for k in range(1, NZ):
+    for k in Z_FAR:
         copy(hz.at[z], hz.at[z], hz_ss.at[0], hz_rs.at[0], zp(k)).start()
     left_here(hz.at[pl.ds(0, NZ - 1)], hz_ss.at[0])
 
@@ -328,16 +361,13 @@
         psum[...] += hit
 
     def vc_copy(p):
-        s = ((x + NX - gray(p)) % NX) * 2 + c
+        s = ((x + NX - GRAY[p]) % NX) * 2 + c
         return copy(xall.at[s], xall.at[s], vc_ss.at[p], vc_rs.at[p], other)
 
-    @pl.loop(0, NX)
-    def _(p):
-        @pl.when(p > 0)
-        def _():
-            vx_copy(gray(p)).wait_recv()
-
-        s = ((x + NX - gray(p)) % NX) * 2
+    for p in range(NX):
+        if p:
+            vx_copy(GRAY[p]).wait_recv()
+        s = ((x + NX - GRAY[p]) % NX) * 2
         vc_copy(p).start()
         first_pass(s + c)
         vc_copy(p).wait_recv()
@@ -380,26 +410,26 @@
     def tx_copy(k):
         return copy(sx.at[k], rx.at[k - 1], tx_ss.at[0], tx_rs.at[0], xp(k))
 
-    @pl.loop(0, NX)
-    def _(p):
-        k = gray((p + 1) % NX)
+    def settle(k):
+        tc_copy(k).wait_recv()
+        t = town[k] + rc[k].astype(F32)
+        if k:
+            sx[k] = t.astype(BF16)
+            tx_copy(k).start()
+        else:
+            town[k] = t
+
+    for p in range(NX):
+        k = GRAY[(p + 1) % NX]
         s = ((x + k) % NX) * 2
         weigh(s + oc)
         weigh(s + c)
         tsrc[k] = spread(s + oc).astype(BF16)
         tc_copy(k).start()
-        t = spread(s + c)
-        tc_copy(k).wait_recv()
-        t = t + rc[k].astype(F32)
-        sx[k] = t.astype(BF16)
-
-        @pl.when(p < NX - 1)
-        def _():
-            tx_copy(k).start()
-
-        @pl.when(p == NX - 1)
-        def _():
-            town[...] = t
+        if p:
+            settle(GRAY[p])
+        town[k] = spread(s + c)
+    settle(0)
 
     acc = dot(gall[0], xall[0], 1, 0)
     for s in range(1, SLOTS):
@@ -423,7 +453,7 @@
         sent.append(tc_copy(k))
     left_here(rx, tx_ss.at[0])
     landed(rx, tx_rs.at[0])
-    t = town[...]
+    t = town[0]
     for k in range(NX - 1):
         t = t + rx[k].astype(F32)
     sg[...] = stack(t).astype(BF16)
@@ -465,7 +495,7 @@
     for k in range(NY - 1):
         q = q + qry[k].astype(F32)
     qz[z] = q.astype(BF16)
-    for k in range(1, NZ):
+    for k in Z_FAR:
         copy(qz.at[z], qz.at[z], qz_ss.at[0], qz_rs.at[0], zp(k)).start()
     left_here(qz.at[pl.ds(0, NZ - 1)], qz_ss.at[0])
 
@@ -478,7 +508,7 @@
 
     ac_cp.wait_recv()
     asx[...] = (aown[core_rows(0, c), :] + arc[...]).reshape(NX, LINE, DOUT)
-    for k in (1, 3, 2):
+    for k in (2, 1, 3):
         copy(asx.at[(x + k) % NX], arx.at[k - 1], ax_ss.at[0], ax_rs.at[0], xp(k)).start()
     flush()
     left_here(arx, ax_ss.at[0])
@@ -556,14 +586,16 @@
     scratch = [
         vm(TOK, DIN), vm(DIN, HID), vm(HID, DOUT), vm(CHUNKS, 4 * SHARD, WIDE), vm(DIN, HID), vm(HID, DOUT),
         vm(NY, HALF, dtype=jnp.int32), vm(PLANE - 1, NY, HALF, dtype=jnp.int32), vm(NY, HALF, 4 * SHARD),
-        vm(CHUNKS, NY, HALF, WIDE), vm(CHUNKS, NY - 1, HALF, WIDE),
-        vm(CHUNKS, NZ, 16, WIDE), vm(CHUNKS, NZ - 1, 16, WIDE), vm(16, HID, dtype=F32),
+        vm(CHUNKS - 1, NY, HALF, WIDE), vm(CHUNKS - 1, NY - 1, HALF, WIDE),
+        vm(CHUNKS - 1, NZ, 16, WIDE), vm(CHUNKS - 1, NZ - 1, 16, WIDE),
+        vm(NZ, NY * 16, WIDE), vm(NZ - 1, NY * 16, WIDE), vm(NY, 16, WIDE), vm(NY - 1, 16, WIDE),
+        vm(16, HID, dtype=F32),
         vm(TOK, HID), vm(TOK, DOUT, dtype=F32), vm(TOK, DOUT),
         vm(SLOTS, BLOCK, DOUT), vm(PLANE, 16, HALF), vm(NZ, 16, 512), vm(NY, 64, ROWS), vm(NY, 64, ROWS),
         vm(SLOTS, TOK, BLOCK, dtype=F32), vm(TOK, HALF, dtype=F32), vm(TOK, HALF, dtype=F32),
         vm(TOK, HALF, dtype=jnp.int32), vm(TOK, HALF, dtype=F32), vm(SLOTS, TOK, BLOCK),
         vm(NX, BLOCK, DOUT), vm(NX, BLOCK, DOUT), vm(NX, BLOCK, DOUT), vm(NX - 1, BLOCK, DOUT),
-        vm(BLOCK, DOUT, dtype=F32), vm(PLANE, 16, HALF), vm(PLANE - 1, 16, HALF),
+        vm(NX, BLOCK, DOUT, dtype=F32), vm(PLANE, 16, HALF), vm(PLANE - 1, 16, HALF),
         vm(PLANE, 16, HALF), vm(HALF, DOUT, dtype=F32), vm(ROWS, DOUT, dtype=F32),
         vm(NX, LINE, DOUT, dtype=F32), vm(NX - 1, LINE, DOUT, dtype=F32),
         vm(HID, DOUT, dtype=F32), vm(NY, HALF, DOUT), vm(NY, HALF, DOUT),
@@ -571,7 +603,7 @@
         vm(NZ, LINE, DOUT),
         vm(NY, NX, 1, HALF, dtype=F32), vm(2, 1, HALF, dtype=F32), vm(SLOTS, 1, BLOCK, dtype=F32),
         pltpu.SemaphoreType.DMA((2 * CHUNKS + 5,)),
-        *dma(1), *dma(2, CHUNKS), *dma(CHUNKS), *dma(CHUNKS),
+        *dma(1), *dma(2, CHUNKS), *dma(CHUNKS - 1), *dma(CHUNKS - 1), *dma(1), *dma(1),
         *dma(1), *dma(3), *dma(4),
         *dma(1), *dma(1),
         *dma(4), *dma(1), *dma(1),

time: 102 us -> 93.5 us (0.917)
  Pallas kernels: 98.3 us -> 89.4 us
    pallas_call x1, Pallas kernels: 98.3 us -> 89.4 us  [local(): pl.pallas_call(kernel, out_shape=(jax.ShapeDtypeStruct((TOK // HALF, HALF...]
where the time goes in v4:
time: 93.5 us; the launch traced here: 93.4 us
  Pallas kernels  89.4 us (96%)
  other arithmetic  2.69 us (3%)
    pallas_call x1, Pallas kernels, local(): pl.pallas_call(kernel, out_shape=(jax.ShapeDtypeStruct((TOK // HALF, HALF...  89.4 us
    mul x1, other arithmetic, scaled(): return grad.reshape(HID, DOUT).astype(F32) * factor  2.69 us

profile of v4, /device:TPU:1, one launch (start us, length us, event | category | flops | bytes accessed | tf_op | source)
XLA Modules:
  0.0 93.4 jit_solution(5288949328789677403)
XLA Ops:
  0.6 89.4 %step.1 = (f32[8,128]{1,0:T(8,128)}, bf16[4,2,4,32,256]{4,3,2,1,0:T(8,128)(2,1)}, bf16[4,2,4,32,256]{4,3,2,1,0:T(8,128)(2,1)}, f32[1,256]{1,0:T(1,128)}) custom-call(s32[32]{0:T(128)} %quo_idx.1, s32[32]{0:T(128)} %rem_idx.1, bf16[1024,1024]{1,0:T(8,128)(2,1)} %feat_hbm.1, bf16[1024,1024]{1,0:T(8,128)(2,1)} %wqi_hbm.1, bf16[1024,256]{1,0:T(8,128)(2,1)} %wqo_hbm.1, ...), custom_call_target="tpu_custom_call" | custom-call | flops 6499999744 | bytes 12000000 | tf_op jit(solution)/shard_map/step/pallas_call | solution.py:615
  90.1 0.0 copy-start
  90.1 2.7 %convert_multiply_fusion = (f32[1024,256]{1,0:T(8,128)}, f32[1024,256]{1,0:T(8,128)}) fusion(bf16[4,2,4,32,256]{4,3,2,1,0:T(8,128)(2,1)} %get-tuple-element.10, f32[256]{0:T(256)} %bitcast.11, bf16[4,2,4,32,256]{4,3,2,1,0:T(8,128)(2,1)} %get-tuple-element.8), kind=kLoop, calls=%fused_computation | loop fusion | flops 1048576 | bytes 3146752 | tf_op jit(solution)/shard_map/mul | solution.py:636
  92.8 0.0 copy-done
  92.8 0.6 copy.15
Async XLA Ops:
  90.1 2.7 %copy-start = (f32[8,128]{1,0:T(8,128)S(1)}, f32[8,128]{1,0:T(8,128)}, u32[]{:S(2)}) copy-start(f32[8,128]{1,0:T(8,128)} %get-tuple-element.7) | copy-start | bytes 12292

commit v5 on v4

--- a/solution.py
+++ b/solution.py
@@ -77,7 +77,7 @@
     est, esum, psum, posb, invb, gall, tsrc, rc, sx, rx, town, sg, rg,
     rgv, arc, aown, asx, arx,
     qfull, qsrc, qrc, qsx, qrx, qsy, qry, qz,
-    nrm, nsum, lc_ref,
+    lc_ref,
     load_sem,
     idx_ss, idx_rs, tab_ss, tab_rs, ry_ss, ry_rs, rz_ss, rz_rs, rf_ss, rf_rs, rl_ss, rl_rs,
     vp_ss, vp_rs, vx_ss, vx_rs, vc_ss, vc_rs,
@@ -86,7 +86,7 @@
     gp_ss, gp_rs,
     ac_ss, ac_rs, ax_ss, ax_rs,
     qc_ss, qc_rs, qx_ss, qx_rs, qy_ss, qy_rs, qz_ss, qz_rs,
-    f_ss, f_rs, fc_ss, fc_rs, n_ss, n_rs, ns_ss, ns_rs,
+    f_ss, f_rs, fc_ss, fc_rs,
 ):
     sec = lax.axis_index("sec")
     dev = lax.axis_index("dev")
@@ -187,9 +187,6 @@
         loads[i].wait()
     pl.semaphore_wait(barrier, greeted)
 
-    for i in range(len(plane)):
-        copy(idx_out, idx_recv.at[i], idx_ss.at[0], idx_rs.at[0], pp(i)).start()
-    left_here(idx_recv, idx_ss.at[0])
     own_rows = pl.ds(pl.multiple_of(c * 2 * SHARD, SHARD), SHARD)
     their_rows = pl.ds(pl.multiple_of(c * 2 * SHARD + SHARD, SHARD), SHARD)
 
@@ -205,6 +202,9 @@
 
     for ch in ORDER:
         tab_copy(ch).start()
+    for i in range(len(plane)):
+        copy(idx_out, idx_recv.at[i], idx_ss.at[0], idx_rs.at[0], pp(i)).start()
+    left_here(idx_recv, idx_ss.at[0])
 
     pos = pos_in[...]
     place = ((pos // 16) % 2) * 1024 + ((pos // 32) % 2) * 512 + ((pos // 8) % 2) * 256
@@ -419,15 +419,15 @@
         else:
             town[k] = t
 
-    for p in range(NX):
-        k = GRAY[(p + 1) % NX]
+    turns = (2, 1, 3, 0)
+    for p, k in enumerate(turns):
         s = ((x + k) % NX) * 2
         weigh(s + oc)
         weigh(s + c)
         tsrc[k] = spread(s + oc).astype(BF16)
         tc_copy(k).start()
         if p:
-            settle(GRAY[p])
+            settle(turns[p - 1])
         town[k] = spread(s + c)
     settle(0)
 
@@ -513,8 +513,9 @@
     flush()
     left_here(arx, ax_ss.at[0])
 
-    def square_sum(v):
-        v = jnp.sum(v * v, axis=0, keepdims=True)
+    def square_sum(m):
+        v = fin[m][...].reshape(HID, DOUT).astype(F32)
+        v = jnp.sum((v * v).reshape(HID // 8, 8, DOUT), axis=0)
         return v[:, :HALF] + v[:, HALF:]
 
     def group(ref, ky, lead):
@@ -549,25 +550,26 @@
         a = a + arx[k]
     fin_item[y, c, x] = a.astype(BF16)
     gather(1)
-    nrm[y, x] = square_sum(q) + square_sum(a)
-    for kx, ky in sheet:
-        copy(nrm.at[y, x], nrm.at[y, x], n_ss.at[ky], n_rs.at[ky], sp(kx, ky)).start()
     gather_core(0)
     flush()
+    for cp in fc_cp:
+        cp.wait_recv()
+    square = square_sum(0)
     gather_core(1)
-    for ky in range(NY):
-        left_here(group(nrm, ky, (0,)), n_ss.at[ky])
-        landed(group(nrm, ky, (0,)), n_rs.at[ky])
-    square = jnp.sum(nrm[...].reshape(NX * NY, HALF), axis=0, keepdims=True)
-    nsum[0] = square
-    ns_cp = push(nsum.at[0], nsum.at[1], ns_ss.at[0], ns_rs.at[0], other)
-    ns_cp.wait_recv()
-    norm = jnp.sqrt(jnp.sum(square + nsum[1], axis=1, keepdims=True))
+    for cp in fc_cp[NY:]:
+        cp.wait_recv()
+    square = square + square_sum(1)
+    square = jnp.sum(square, axis=0, keepdims=True)
+    norm = jnp.sqrt(jnp.sum(square, axis=1, keepdims=True))
     limit = (HID * DOUT / 2) ** 0.5
     factor_ref[...] = jnp.broadcast_to(limit / jnp.maximum(norm, limit), (1, DOUT))
-    for cp in fc_cp:
-        cp.wait_recv()
     flush()
+
+
+def finish(loss_in, query_in, item_in, factor_in, loss_out, query_out, item_out):
+    loss_out[...] = loss_in[...]
+    query_out[...] = query_in[...].reshape(HID, DOUT).astype(F32) * factor_in[...]
+    item_out[...] = item_in[...].reshape(HID, DOUT).astype(F32) * factor_in[...]
 
 
 def local(
@@ -601,7 +603,7 @@
         vm(HID, DOUT, dtype=F32), vm(NY, HALF, DOUT), vm(NY, HALF, DOUT),
         vm(NX, NY, LINE, DOUT), vm(NX - 1, NY, LINE, DOUT), vm(NY, LINE, DOUT), vm(NY - 1, LINE, DOUT),
         vm(NZ, LINE, DOUT),
-        vm(NY, NX, 1, HALF, dtype=F32), vm(2, 1, HALF, dtype=F32), vm(SLOTS, 1, BLOCK, dtype=F32),
+        vm(SLOTS, 1, BLOCK, dtype=F32),
         pltpu.SemaphoreType.DMA((2 * CHUNKS + 5,)),
         *dma(1), *dma(2, CHUNKS), *dma(CHUNKS - 1), *dma(CHUNKS - 1), *dma(1), *dma(1),
         *dma(1), *dma(3), *dma(4),
@@ -610,7 +612,7 @@
         *dma(1),
         *dma(1), *dma(1),
         *dma(1), *dma(1), *dma(1), *dma(1),
-        *dma(2, 4), *dma(2, 4), *dma(4), *dma(1),
+        *dma(2, 4), *dma(2, 4),
     ]
     losses, grad_query, grad_item, factor = pl.pallas_call(
         kernel,
@@ -632,10 +634,18 @@
         quo_bucket, rem_bucket, user_features, w_query_in, w_query_out, quo_table, rem_table, w_item_in,
         w_item_out, counts.reshape(16, HALF), positive.reshape(TOK // HALF, HALF),
     )
-    def scaled(grad):
-        return grad.reshape(HID, DOUT).astype(F32) * factor
-
-    return (losses.reshape(TOK), scaled(grad_query), scaled(grad_item))
+    losses, grad_query, grad_item = pl.pallas_call(
+        finish,
+        out_shape=(
+            jax.ShapeDtypeStruct((TOK // HALF, HALF), F32),
+            jax.ShapeDtypeStruct((HID, DOUT), F32),
+            jax.ShapeDtypeStruct((HID, DOUT), F32),
+        ),
+        in_specs=[vmem] * 4,
+        out_specs=(vmem, vmem, vmem),
+        name="scale",
+    )(losses, grad_query, grad_item, factor)
+    return (losses.reshape(TOK), grad_query, grad_item)
 
 
 def solution(mesh):

time: 93.5 us -> 90.8 us (0.971)
  other arithmetic: 2.69 us -> 0 us
    mul x1 -> x0, other arithmetic: 2.69 us -> none  [scaled(): return grad.reshape(HID, DOUT).astype(F32) * factor]
    pallas_call x0 -> x1, Pallas kernels: none -> 2.59 us  [local(): pl.pallas_call(finish, out_shape=(jax.ShapeDtypeStruct((TOK // HALF, HALF...]
    pallas_call x1, Pallas kernels: 89.4 us -> 87.5 us  [local(): pl.pallas_call(kernel, out_shape=(jax.ShapeDtypeStruct((TOK // HALF, HALF...]
where the time goes in v5:
time: 90.8 us; the launch traced here: 90.7 us
  Pallas kernels  90.1 us (99%)
    pallas_call x1, Pallas kernels, local(): pl.pallas_call(kernel, out_shape=(jax.ShapeDtypeStruct((TOK // HALF, HALF...  87.5 us
    pallas_call x1, Pallas kernels, local(): pl.pallas_call(finish, out_shape=(jax.ShapeDtypeStruct((TOK // HALF, HALF...  2.59 us

profile of v5, /device:TPU:1, one launch (start us, length us, event | category | flops | bytes accessed | tf_op | source)
XLA Modules:
  0.0 90.7 jit_solution(2743768611561877616)
XLA Ops:
  0.6 87.5 %step.1 = (f32[8,128]{1,0:T(8,128)}, bf16[4,2,4,32,256]{4,3,2,1,0:T(8,128)(2,1)}, bf16[4,2,4,32,256]{4,3,2,1,0:T(8,128)(2,1)}, f32[1,256]{1,0:T(1,128)}) custom-call(s32[32]{0:T(128)} %quo_idx.1, s32[32]{0:T(128)} %rem_idx.1, bf16[1024,1024]{1,0:T(8,128)(2,1)} %feat_hbm.1, bf16[1024,1024]{1,0:T(8,128)(2,1)} %wqi_hbm.1, bf16[1024,256]{1,0:T(8,128)(2,1)} %wqo_hbm.1, ...), custom_call_target="tpu_custom_call" | custom-call | flops 6499999744 | bytes 12000000 | tf_op jit(solution)/shard_map/step/pallas_call | solution.py:617
  88.1 2.6 %scale.1 = (f32[8,128]{1,0:T(8,128)}, f32[1024,256]{1,0:T(8,128)}, f32[1024,256]{1,0:T(8,128)}) custom-call(f32[8,128]{1,0:T(8,128)} %get-tuple-element.10.loss_in, bf16[4,2,4,32,256]{4,3,2,1,0:T(8,128)(2,1)} %get-tuple-element.11.query_in, bf16[4,2,4,32,256]{4,3,2,1,0:T(8,128)(2,1)} %get-tuple-element.12.item_in, f32[1,256]{1,0:T(1,128)} %get-tuple-element.13.factor_in), custom_call_target="tpu_custom_call" | custom-call | tf_op jit(solution)/shard_map/scale/pallas_call | solution.py:637

commit v6 on v5

--- a/solution.py
+++ b/solution.py
@@ -69,9 +69,10 @@
 
 
 def kernel(
-    quo_idx, rem_idx, feat_hbm, wqi_hbm, wqo_hbm, quo_hbm, rem_hbm, wii_hbm, wio_hbm, counts_in, pos_in,
+    quo_idx_hbm, rem_idx_hbm, feat_hbm, wqi_hbm, wqo_hbm, quo_hbm, rem_hbm, wii_hbm, wio_hbm, counts_hbm,
+    pos_hbm,
     loss_ref, fin_query, fin_item, factor_ref,
-    feat, wqi, wqo, tab, wii, wio,
+    quo_idx, rem_idx, counts_in, pos_in, feat, wqi, wqo, tab, wii, wio,
     idx_out, idx_recv, sel, srow, rrow, zrow, rzrow, srz, rrz, sry, rry, pre,
     hq, qraw, qv, xall, gv, hz, hsrc, hcol,
     est, esum, psum, posb, invb, gall, tsrc, rc, sx, rx, town, sg, rg,
@@ -169,22 +170,28 @@
         cp = pltpu.make_async_copy(src, dst, load_sem.at[len(loads)])
         cp.start()
         loads.append(cp)
-
+        return cp
+
+    first = [load(quo_idx_hbm, quo_idx), load(rem_idx_hbm, rem_idx)]
+    shards = []
     for ch in range(CHUNKS):
-        load(quo_hbm.at[:, ch * WIDE : (ch + 1) * WIDE], tab.at[ch, pl.ds(0, SHARD)])
-        load(rem_hbm.at[:, ch * WIDE : (ch + 1) * WIDE], tab.at[ch, pl.ds(2 * SHARD, SHARD)])
-    for src, dst in ((feat_hbm, feat), (wqi_hbm, wqi), (wqo_hbm, wqo), (wii_hbm, wii), (wio_hbm, wio)):
-        load(src, dst)
+        shards.append(load(quo_hbm.at[:, ch * WIDE : (ch + 1) * WIDE], tab.at[ch, pl.ds(0, SHARD)]))
+        shards.append(load(rem_hbm.at[:, ch * WIDE : (ch + 1) * WIDE], tab.at[ch, pl.ds(2 * SHARD, SHARD)]))
+    small = [load(pos_hbm, pos_in), load(counts_hbm, counts_in)]
+    matrices = ((feat_hbm, feat), (wqi_hbm, wqi), (wqo_hbm, wqo), (wii_hbm, wii), (wio_hbm, wio))
+    large = [load(src, dst) for src, dst in matrices]
 
     lane = lax.broadcasted_iota(jnp.int32, (NY, HALF), 1) - z * 2 * QUARTER
     lane = jnp.where(lax.broadcasted_iota(jnp.int32, (NY, HALF), 0) == y, lane, -1)
+    for cp in first:
+        cp.wait()
     asked = jnp.zeros((NY, HALF), jnp.int32)
     for j in range(QUARTER):
         asked = jnp.where(lane == j, quo_idx[sec * QUARTER + j], asked)
         asked = jnp.where(lane == QUARTER + j, rem_idx[sec * QUARTER + j] + TROWS, asked)
     idx_out[...] = asked
-    for i in range(2 * CHUNKS):
-        loads[i].wait()
+    for cp in shards:
+        cp.wait()
     pl.semaphore_wait(barrier, greeted)
 
     own_rows = pl.ds(pl.multiple_of(c * 2 * SHARD, SHARD), SHARD)
@@ -206,6 +213,8 @@
         copy(idx_out, idx_recv.at[i], idx_ss.at[0], idx_rs.at[0], pp(i)).start()
     left_here(idx_recv, idx_ss.at[0])
 
+    for cp in small:
+        cp.wait()
     pos = pos_in[...]
     place = ((pos // 16) % 2) * 1024 + ((pos // 32) % 2) * 512 + ((pos // 8) % 2) * 256
     place = place + ((pos // 64) % 4) * 64 + (pos // 256) * 8 + pos % 8
@@ -227,8 +236,8 @@
         wide = dot(high, pick, 1, 0) * 8.0 + dot(low, pick, 1, 0)
         lc_ref[s] = jnp.log(jnp.sum(jnp.where(keep, wide, 0.0), axis=0, keepdims=True)) * LOG2E
 
-    loads[2 * CHUNKS].wait()
-    loads[2 * CHUNKS + 1].wait()
+    large[0].wait()
+    large[1].wait()
 
     hq[...] = jnp.maximum(dot(feat[...], wqi[...], 1, 0), 0.0).astype(BF16)
 
@@ -264,13 +273,13 @@
         else:
             for k in (2, 1, 3, 0):
                 srow[ch, k] = dot(sel[(y + k) % NY], tab[ch], 1, 0).astype(BF16)
-                if k:
+                if k and ch != 2:
                     row_copy(ch, k).start()
             left_here(rrow.at[ch], ry_ss.at[ch])
         sent.append(tab_copy(ch))
         sent.append(tab_core_copy(ch))
 
-    loads[2 * CHUNKS + 2].wait()
+    large[2].wait()
 
     raw = dot(hq[...], wqo[...], 1, 0)
     qraw[...] = raw
@@ -283,6 +292,9 @@
 
     def along_z(ch):
         landed(rrow.at[ch], ry_rs.at[ch])
+        if ch == 0:
+            for k in (2, 1, 3):
+                row_copy(2, k).start()
         s = srow[ch, 0].astype(F32)
         for k in range(NY - 1):
             s = s + rrow[ch, k].astype(F32)
@@ -303,8 +315,8 @@
     left_here(rry, rl_ss.at[0])
     along_z(2)
 
-    loads[2 * CHUNKS + 3].wait()
-    loads[2 * CHUNKS + 4].wait()
+    large[3].wait()
+    large[4].wait()
     pre[...] = jnp.zeros_like(pre)
 
     for ch in (0, 1, ZFIRST, 2):
@@ -373,24 +385,8 @@
         vc_copy(p).wait_recv()
         first_pass(s + oc)
 
-    landed(hz.at[pl.ds(0, NZ - 1)], hz_rs.at[0])
-    hv = hz[...].astype(F32)
-    hv = jnp.concatenate([hv[:, :8, :].reshape(64, 512), hv[:, 8:, :].reshape(64, 512)], axis=1)
-    hv = hv.astype(BF16)
-    for i in range(NY):
-        hsrc[i] = hv[:, i * ROWS : (i + 1) * ROWS]
-    hcol[y] = hsrc[y]
-    for k in range(1, NY):
-        copy(hsrc.at[(y + k) % NY], hcol.at[y], hy_ss.at[0], hy_rs.at[0], yp(k)).start()
-    left_here(hcol.at[pl.ds(0, NY - 1)], hy_ss.at[0])
     sums = jnp.sum(esum[...], axis=1, keepdims=True)
-    picked = jnp.sum(psum[...], axis=1, keepdims=True)
     invb[...] = jnp.broadcast_to(1.0 / sums, (TOK, HALF))
-    loss = (jnp.log2(sums) - picked) * (1.0 / LOG2E)
-    loss = jnp.broadcast_to(loss, (TOK, HALF)).reshape(TOK // HALF, HALF, HALF)
-    down = lax.broadcasted_iota(jnp.int32, (TOK // HALF, HALF, HALF), 1)
-    across = lax.broadcasted_iota(jnp.int32, (TOK // HALF, HALF, HALF), 2)
-    loss_ref[...] = jnp.sum(jnp.where(down == across, loss, 0.0), axis=1)
 
     def weigh(s):
         lanes = lax.broadcasted_iota(jnp.int32, (TOK, HALF), 1)
@@ -435,6 +431,24 @@
     for s in range(1, SLOTS):
         acc = acc + dot(gall[s], xall[s], 1, 0)
     qv[...] = norm_vjp(qraw[...], acc * INV_TEMPER).astype(BF16)
+
+    landed(hz.at[pl.ds(0, NZ - 1)], hz_rs.at[0])
+    hv = hz[...].astype(F32)
+    hv = jnp.concatenate([hv[:, :8, :].reshape(64, 512), hv[:, 8:, :].reshape(64, 512)], axis=1)
+    hv = hv.astype(BF16)
+    for i in range(NY):
+        hsrc[i] = hv[:, i * ROWS : (i + 1) * ROWS]
+    hcol[y] = hsrc[y]
+    for k in range(1, NY):
+        copy(hsrc.at[(y + k) % NY], hcol.at[y], hy_ss.at[0], hy_rs.at[0], yp(k)).start()
+    left_here(hcol.at[pl.ds(0, NY - 1)], hy_ss.at[0])
+    picked = jnp.sum(psum[...], axis=1, keepdims=True)
+    sums = jnp.sum(esum[...], axis=1, keepdims=True)
+    loss = (jnp.log2(sums) - picked) * (1.0 / LOG2E)
+    loss = jnp.broadcast_to(loss, (TOK, HALF)).reshape(TOK // HALF, HALF, HALF)
+    down = lax.broadcasted_iota(jnp.int32, (TOK // HALF, HALF, HALF), 1)
+    across = lax.broadcasted_iota(jnp.int32, (TOK // HALF, HALF, HALF), 2)
+    loss_ref[...] = jnp.sum(jnp.where(down == across, loss, 0.0), axis=1)
 
     qfull[...] = dot(hq[...], qv[...], 0, 0)
 
@@ -584,8 +598,9 @@
 
     anyspace = pl.BlockSpec(memory_space=pl.ANY)
     vmem = pl.BlockSpec(memory_space=pltpu.VMEM)
-    smem = pl.BlockSpec(memory_space=pltpu.SMEM)
     scratch = [
+        pltpu.SMEM((BLOCK // 8,), jnp.int32), pltpu.SMEM((BLOCK // 8,), jnp.int32),
+        vm(16, HALF, dtype=jnp.int32), vm(TOK // HALF, HALF, dtype=jnp.int32),
         vm(TOK, DIN), vm(DIN, HID), vm(HID, DOUT), vm(CHUNKS, 4 * SHARD, WIDE), vm(DIN, HID), vm(HID, DOUT),
         vm(NY, HALF, dtype=jnp.int32), vm(PLANE - 1, NY, HALF, dtype=jnp.int32), vm(NY, HALF, 4 * SHARD),
         vm(CHUNKS - 1, NY, HALF, WIDE), vm(CHUNKS - 1, NY - 1, HALF, WIDE),
@@ -604,7 +619,7 @@
         vm(NX, NY, LINE, DOUT), vm(NX - 1, NY, LINE, DOUT), vm(NY, LINE, DOUT), vm(NY - 1, LINE, DOUT),
         vm(NZ, LINE, DOUT),
         vm(SLOTS, 1, BLOCK, dtype=F32),
-        pltpu.SemaphoreType.DMA((2 * CHUNKS + 5,)),
+        pltpu.SemaphoreType.DMA((2 * CHUNKS + 9,)),
         *dma(1), *dma(2, CHUNKS), *dma(CHUNKS - 1), *dma(CHUNKS - 1), *dma(1), *dma(1),
         *dma(1), *dma(3), *dma(4),
         *dma(1), *dma(1),
@@ -622,7 +637,7 @@
             jax.ShapeDtypeStruct((NY, NC, NX, LINE, DOUT), BF16),
             jax.ShapeDtypeStruct((1, DOUT), F32),
         ),
-        in_specs=[smem] * 2 + [anyspace] * 7 + [vmem] * 2,
+        in_specs=[anyspace] * 11,
         out_specs=(vmem, vmem, vmem, vmem),
         scratch_shapes=scratch,
         compiler_params=pltpu.CompilerParams(

time: 90.8 us -> 90.7 us (level)
  no operation moved by 1% of the time
where the time goes in v6:
time: 90.7 us; the launch traced here: 90.6 us
  Pallas kernels  89.9 us (99%)
    pallas_call x1, Pallas kernels, local(): pl.pallas_call(kernel, out_shape=(jax.ShapeDtypeStruct((TOK // HALF, HALF...  87.3 us
    pallas_call x1, Pallas kernels, local(): pl.pallas_call(finish, out_shape=(jax.ShapeDtypeStruct((TOK // HALF, HALF...  2.59 us

profile of v6, /device:TPU:1, one launch (start us, length us, event | category | flops | bytes accessed | tf_op | source)
XLA Modules:
  0.0 90.6 jit_solution(6083482325635274660)
XLA Ops:
  0.6 87.3 %step.1 = (f32[8,128]{1,0:T(8,128)}, bf16[4,2,4,32,256]{4,3,2,1,0:T(8,128)(2,1)}, bf16[4,2,4,32,256]{4,3,2,1,0:T(8,128)(2,1)}, f32[1,256]{1,0:T(1,128)}) custom-call(s32[32]{0:T(128)} %quo_idx_hbm.1, s32[32]{0:T(128)} %rem_idx_hbm.1, bf16[1024,1024]{1,0:T(8,128)(2,1)} %feat_hbm.1, bf16[1024,1024]{1,0:T(8,128)(2,1)} %wqi_hbm.1, bf16[1024,256]{1,0:T(8,128)(2,1)} %wqo_hbm.1, ...), custom_call_target="tpu_custom_call" | custom-call | flops 6499999744 | bytes 12000000 | tf_op jit(solution)/shard_map/step/pallas_call | solution.py:632
  88.0 2.6 %scale.1 = (f32[8,128]{1,0:T(8,128)}, f32[1024,256]{1,0:T(8,128)}, f32[1024,256]{1,0:T(8,128)}) custom-call(f32[8,128]{1,0:T(8,128)} %get-tuple-element.10.loss_in, bf16[4,2,4,32,256]{4,3,2,1,0:T(8,128)(2,1)} %get-tuple-element.11.query_in, bf16[4,2,4,32,256]{4,3,2,1,0:T(8,128)(2,1)} %get-tuple-element.12.item_in, f32[1,256]{1,0:T(1,128)} %get-tuple-element.13.factor_in), custom_call_target="tpu_custom_call" | custom-call | tf_op jit(solution)/shard_map/scale/pallas_call | solution.py:652
